TPU v7x, 128 devices: a whole 4x4x4 slice. The times are simulated.
128 devices in a mesh: dp: 2 (over z_hi), seq: 32 (over y, x, z_lo), tp: 2 (over core).
Axes of the slice: x: 4, y: 4, z: 4 (z_hi: 2, z_lo: 2; z = z_hi * 2 + z_lo), core: 2. Of those that a mesh axis runs over, the one named last changes fastest.
Arguments:
- bases: int32 [2, 49152], P('dp', 'seq'), may hold values from -2147483648 to 2147483646
- shifts: int32 [2], P('dp'), may hold values from -6144 to 6144
- embed_weight: bfloat16 [512, 768], replicated, may hold values from -0.5 to 0.5
- conv_weight: bfloat16 [5, 768, 1536], P(None, None, 'tp'), may hold values from -0.09375 to 0.09375
- query_weight: bfloat16 [1536, 1536], P(None, 'tp'), may hold values from -0.15625 to 0.15625
- keyvalue_weight: bfloat16 [1536, 2, 256], P(None, 'tp'), may hold values from -0.15625 to 0.15625
- output_weight: bfloat16 [1536, 1536], P('tp'), may hold values from -0.15625 to 0.15625
- slopes: float32 [12], P('tp'), may hold values from 0.1 to 16
- cotangent: bfloat16 [2, 6144, 1536], P('dp', 'seq', 'tp'), may hold values from -6 to 6
Outputs:
- result: bfloat16 [2, 6144, 1536], P('dp', 'seq', 'tp')
- grad_embed: float32 [512, 768], P('seq')
- grad_conv: float32 [5, 768, 1536], P(None, 'seq', 'tp')
- grad_query: float32 [1536, 1536], P('seq', 'tp')
- grad_keyvalue: float32 [1536, 2, 256], P('seq', 'tp')
- grad_output: float32 [1536, 1536], P('tp', 'seq')
Inputs may be any that keep to these rules, and one draw needn't show every extreme that they name: Word w of a sample holds the sample's bases 16 w to 16 w + 15; base 16 w + r is the two-bit field at bits 2 r and 2 r + 1 of the word's two's-complement pattern, 0 to 3 standing for A, C, G, T.
All inputs are finite; a program needn't handle non-finite values.
Results may differ from a plain program's by a relative error of at most 0.039.
Values may be sent and summed in bfloat16 or wider, within the bound.
A program may use at most 128 MiB of HBM per device.

v0:
```python
import math

import jax
import jax.numpy as jnp
from jax import lax
from jax.sharding import PartitionSpec as P

ROOT_TWO_PI = math.sqrt(2.0 / math.pi)
CUBIC = 0.044715
EPSILON = 1e-06
DISTANCE_SCALE = 128.0


def padded_2(shard, sides, width):
    for axis, dim in sides:
        size, length = (lax.axis_size(axis), shard.shape[dim])
        up = [(i, (i + 1) % size) for i in range(size - 1)]
        down = [(j, i) for i, j in up]
        last = lax.slice_in_dim(shard, length - width, length, axis=dim)
        first = lax.slice_in_dim(shard, 0, width, axis=dim)
        before = lax.ppermute(last, axis, up)
        after = lax.ppermute(first, axis, down)
        shard = jnp.concatenate([before, shard, after], axis=dim)
    return shard


def gelu_value(inputs):
    return (
        0.5 * inputs * (1.0 + jnp.tanh(ROOT_TWO_PI * (inputs + CUBIC * inputs * inputs * inputs)))
    )


def gelu_slope(inputs):
    inner = jnp.tanh(ROOT_TWO_PI * (inputs + CUBIC * inputs * inputs * inputs))
    return 0.5 * (1.0 + inner) + 0.5 * inputs * (1.0 - inner * inner) * ROOT_TWO_PI * (
        1.0 + 3.0 * CUBIC * inputs * inputs
    )


def inverse_rms(values):
    return lax.rsqrt(jnp.mean(values * values, axis=-1, keepdims=True) + EPSILON)


def unpack_local(packed, bases_tok):
    shift_bits = 2 * jnp.arange(16, dtype=jnp.int32)
    fields = jnp.right_shift(packed[:, None], shift_bits) & 3
    letters = fields.reshape(-1, bases_tok)
    onehot = letters[..., None] == jnp.arange(4, dtype=jnp.int32)
    return onehot.reshape(letters.shape[0], 4 * bases_tok).astype(jnp.bfloat16)


def sequence_rims(values, reach_rows):
    return padded_2(values, (("seq", 0),), reach_rows)


def feature_halves(values):
    return lax.all_gather(values, "tp", axis=1, tiled=True)


def score_block(grouped_query, key_piece, slope_table, query_pos, first_key, offset, head_dim):
    piece_rows = key_piece.shape[0]
    local_groups = slope_table.shape[0]
    paired = key_piece.reshape(piece_rows, local_groups, 2 * head_dim)
    keys_now = paired[:, :, :head_dim]
    values_now = paired[:, :, head_dim:]
    scores = jnp.einsum(
        "qgmd,kgd->qgmk", grouped_query, keys_now, preferred_element_type=jnp.float32
    ) / math.sqrt(head_dim)
    key_pos = first_key + jnp.arange(piece_rows, dtype=jnp.int32)
    distance = jnp.abs(query_pos[:, None] - key_pos[None, :] + offset).astype(jnp.float32)
    scores = scores - slope_table[None, :, :, None] * distance[:, None, None, :] / DISTANCE_SCALE
    return (scores, keys_now, values_now)


def spread_order(values, axis_dim, seq_count, data_count):
    shape_now = values.shape
    parted = values.reshape(
        shape_now[:axis_dim]
        + (seq_count, data_count, shape_now[axis_dim] // (seq_count * data_count))
        + shape_now[axis_dim + 1 :]
    )
    return jnp.swapaxes(parted, axis_dim, axis_dim + 1).reshape(shape_now)


def per_device(
    bases,
    shifts,
    embed_weight,
    conv_weight,
    query_weight,
    keyvalue_weight,
    output_weight,
    slopes,
    cotangent,
):
    tokens = cotangent.shape[1]
    conv_in = embed_weight.shape[1]
    bases_tok = embed_weight.shape[0] // 4
    taps_count = conv_weight.shape[0]
    reach_rows = taps_count // 2
    local_out = conv_weight.shape[2]
    width_all = query_weight.shape[0]
    local_groups = keyvalue_weight.shape[1]
    head_dim = keyvalue_weight.shape[2] // 2
    local_heads = slopes.shape[0]
    members = local_heads // local_groups
    slope_table = slopes.reshape(local_groups, members)
    offset = shifts[0]
    query_pos = lax.axis_index("seq") * tokens + jnp.arange(tokens, dtype=jnp.int32)
    patches = unpack_local(bases[0], bases_tok)
    embedded = jnp.dot(patches, embed_weight, preferred_element_type=jnp.float32).astype(
        jnp.bfloat16
    )
    embedded_wide = embedded.astype(jnp.float32)
    scale_in = inverse_rms(embedded_wide)
    normed_in = embedded_wide * scale_in
    activated = gelu_value(normed_in).astype(jnp.bfloat16)
    padded = sequence_rims(activated, reach_rows)
    windows = jnp.concatenate(
        [padded[tap_index : tap_index + tokens] for tap_index in range(taps_count)], axis=-1
    )
    convolved = jnp.dot(
        windows,
        conv_weight.reshape(taps_count * conv_in, local_out),
        preferred_element_type=jnp.float32,
    )
    hidden = (convolved + embedded_wide).astype(jnp.bfloat16)
    hidden_full = feature_halves(hidden).astype(jnp.float32)
    scale_mid = inverse_rms(hidden_full)
    normed_wide = hidden_full * scale_mid
    normed = normed_wide.astype(jnp.bfloat16)
    queries = jnp.dot(normed, query_weight, preferred_element_type=jnp.float32).astype(jnp.bfloat16)
    pair_weight = keyvalue_weight.reshape(width_all, local_groups * 2 * head_dim)
    keyvalue = jnp.dot(normed, pair_weight, preferred_element_type=jnp.float32).astype(jnp.bfloat16)
    grouped_query = queries.reshape(tokens, local_groups, members, head_dim)

    def absorb_block(running, key_piece, first_key):
        highest, totals, mixed_sum = running
        scores, keys_now, values_now = score_block(
            grouped_query, key_piece, slope_table, query_pos, first_key, offset, head_dim
        )
        newest = jnp.maximum(highest, jnp.max(scores, axis=-1))
        fading = jnp.exp(highest - newest)
        weights = jnp.exp(scores - newest[..., None])
        totals = totals * fading + jnp.sum(weights, axis=-1)
        mixed_sum = mixed_sum * fading[..., None] + jnp.einsum(
            "qgmk,kgd->qgmd",
            weights.astype(jnp.bfloat16),
            values_now,
            preferred_element_type=jnp.float32,
        )
        return (newest, totals, mixed_sum)

    start_state = (
        jnp.full((tokens, local_groups, members), -1e30, jnp.float32),
        jnp.zeros((tokens, local_groups, members), jnp.float32),
        jnp.zeros((tokens, local_groups, members, head_dim), jnp.float32),
    )
    key_rows = lax.all_gather(keyvalue, "seq", axis=0, tiled=True)
    piece_rows = key_rows.shape[0]
    blocked = key_rows.reshape(piece_rows // 512, 512, key_rows.shape[1])
    block_firsts = 512 * jnp.arange(piece_rows // 512, dtype=jnp.int32)

    def scan_step(carried, inputs_now):
        return (absorb_block(carried, inputs_now[0], inputs_now[1]), None)

    final_state, unused = lax.scan(scan_step, start_state, (blocked, block_firsts))
    running = final_state
    highest, totals, mixed_sum = running
    attended_grouped = (mixed_sum / totals[..., None]).astype(jnp.bfloat16)
    log_totals = highest + jnp.log(totals)
    attended = attended_grouped.reshape(tokens, local_heads * head_dim)
    partial_out = jnp.dot(attended, output_weight, preferred_element_type=jnp.float32)
    projected = lax.psum_scatter(
        partial_out.astype(jnp.bfloat16), "tp", scatter_dimension=1, tiled=True
    ).astype(jnp.float32)
    result = (hidden.astype(jnp.float32) + projected).astype(jnp.bfloat16)
    cotangent_local = cotangent[0]
    cotangent_full = feature_halves(cotangent_local)
    grad_output = jnp.einsum(
        "tq,tc->qc", attended, cotangent_full, preferred_element_type=jnp.float32
    )
    back_attended = jnp.einsum(
        "tc,qc->tq", cotangent_full, output_weight, preferred_element_type=jnp.float32
    ).astype(jnp.bfloat16)
    back_grouped = back_attended.reshape(tokens, local_groups, members, head_dim)
    deltas = jnp.sum(
        back_grouped.astype(jnp.float32) * attended_grouped.astype(jnp.float32), axis=-1
    )
    total_rows = key_rows.shape[0]
    block_rows = 512
    block_count = total_rows // block_rows
    key_blocked = key_rows.reshape(block_count, block_rows, key_rows.shape[1])
    key_firsts = block_rows * jnp.arange(block_count, dtype=jnp.int32)

    def back_block(query_grad, inputs_now):
        scores, keys_now, values_now = score_block(
            grouped_query, inputs_now[0], slope_table, query_pos, inputs_now[1], offset, head_dim
        )
        probs = jnp.exp(scores - log_totals[..., None])
        value_grad = jnp.einsum(
            "qgmk,qgmd->kgd",
            probs.astype(jnp.bfloat16),
            back_grouped,
            preferred_element_type=jnp.float32,
        )
        back_probs = jnp.einsum(
            "qgmd,kgd->qgmk", back_grouped, values_now, preferred_element_type=jnp.float32
        )
        grad_scores = (probs * (back_probs - deltas[..., None]) / math.sqrt(head_dim)).astype(
            jnp.bfloat16
        )
        query_grad = query_grad + jnp.einsum(
            "qgmk,kgd->qgmd", grad_scores, keys_now, preferred_element_type=jnp.float32
        )
        key_grad = jnp.einsum(
            "qgmk,qgmd->kgd", grad_scores, grouped_query, preferred_element_type=jnp.float32
        )
        return (query_grad, jnp.concatenate([key_grad, value_grad], axis=-1))

    query_start = jnp.zeros((tokens, local_groups, members, head_dim), jnp.float32)
    query_total, pair_blocks = lax.scan(back_block, query_start, (key_blocked, key_firsts))
    back_query = query_total.astype(jnp.bfloat16).reshape(tokens, local_heads * head_dim)
    pair_partial = pair_blocks.reshape(total_rows, local_groups * 2 * head_dim)
    back_pair = lax.psum_scatter(
        pair_partial.astype(jnp.bfloat16), "seq", scatter_dimension=0, tiled=True
    )
    grad_query = jnp.einsum("tc,tq->cq", normed, back_query, preferred_element_type=jnp.float32)
    grad_pair = jnp.einsum(
        "tc,tq->cq", normed, back_pair, preferred_element_type=jnp.float32
    ).reshape(width_all, local_groups, 2 * head_dim)
    normed_partial = jnp.einsum(
        "tq,cq->tc", back_query, query_weight, preferred_element_type=jnp.float32
    )
    normed_partial = normed_partial + jnp.einsum(
        "tq,cq->tc", back_pair, pair_weight, preferred_element_type=jnp.float32
    )
    back_normed = lax.psum(normed_partial.astype(jnp.bfloat16), "tp").astype(jnp.float32)
    back_wide = scale_mid * (
        back_normed - normed_wide * jnp.mean(back_normed * normed_wide, axis=-1, keepdims=True)
    )
    back_hidden = cotangent_local.astype(jnp.float32) + lax.dynamic_slice_in_dim(
        back_wide, lax.axis_index("tp") * local_out, local_out, 1
    )
    back_conv = back_hidden.astype(jnp.bfloat16)
    grad_conv = jnp.einsum(
        "tw,to->wo", windows, back_conv, preferred_element_type=jnp.float32
    ).reshape(taps_count, conv_in, local_out)
    back_padded = sequence_rims(back_conv, reach_rows)
    back_windows = jnp.concatenate(
        [
            back_padded[taps_count - 1 - tap_index : taps_count - 1 - tap_index + tokens]
            for tap_index in range(taps_count)
        ],
        axis=-1,
    )
    active_partial = jnp.einsum(
        "tko,kco->tc",
        back_windows.reshape(tokens, taps_count, local_out),
        conv_weight,
        preferred_element_type=jnp.float32,
    )
    back_active, back_residual = (
        lax.psum(active_partial.astype(jnp.bfloat16), "tp").astype(jnp.float32),
        lax.psum(back_hidden.astype(jnp.bfloat16), "tp").astype(jnp.float32),
    )
    back_normed_in = back_active * gelu_slope(normed_in)
    back_embedded = back_residual + scale_in * (
        back_normed_in - normed_in * jnp.mean(back_normed_in * normed_in, axis=-1, keepdims=True)
    )
    back_embedded = back_embedded.astype(jnp.bfloat16)
    grad_embed = jnp.einsum("tp,tc->pc", patches, back_embedded, preferred_element_type=jnp.float32)
    seq_count = lax.axis_size("seq")
    data_count = lax.axis_size("dp")
    spread = (
        spread_order(grad_embed, 0, seq_count, data_count),
        spread_order(grad_conv, 1, seq_count, data_count),
        spread_order(grad_query, 0, seq_count, data_count),
        spread_order(grad_pair, 0, seq_count, data_count),
        spread_order(grad_output, 1, seq_count, data_count),
    )
    pieces = (
        lax.psum_scatter(spread[0], ("dp", "seq"), scatter_dimension=0, tiled=True),
        lax.psum_scatter(spread[1], ("dp", "seq"), scatter_dimension=1, tiled=True),
        lax.psum_scatter(spread[2], ("dp", "seq"), scatter_dimension=0, tiled=True),
        lax.psum_scatter(spread[3], ("dp", "seq"), scatter_dimension=0, tiled=True),
        lax.psum_scatter(spread[4], ("dp", "seq"), scatter_dimension=1, tiled=True),
    )
    summed = (
        lax.all_gather(pieces[0].astype(jnp.bfloat16), "dp", axis=0, tiled=True).astype(
            jnp.float32
        ),
        lax.all_gather(pieces[1].astype(jnp.bfloat16), "dp", axis=1, tiled=True).astype(
            jnp.float32
        ),
        lax.all_gather(pieces[2].astype(jnp.bfloat16), "dp", axis=0, tiled=True).astype(
            jnp.float32
        ),
        lax.all_gather(pieces[3].astype(jnp.bfloat16), "dp", axis=0, tiled=True).astype(
            jnp.float32
        ),
        lax.all_gather(pieces[4].astype(jnp.bfloat16), "dp", axis=1, tiled=True).astype(
            jnp.float32
        ),
    )
    factor = (data_count * seq_count * tokens) ** (-0.5)
    return (
        result[None],
        summed[0] * factor,
        summed[1] * factor,
        summed[2] * factor,
        summed[3] * factor,
        summed[4] * factor,
    )


def solution(mesh):
    placed = (
        P("dp", "seq"),
        P("dp"),
        P(),
        P(None, None, "tp"),
        P(None, "tp"),
        P(None, "tp", None),
        P("tp", None),
        P("tp"),
        P("dp", "seq", "tp"),
    )
    return jax.shard_map(
        per_device,
        mesh=mesh,
        in_specs=placed,
        out_specs=(
            P("dp", "seq", "tp"),
            P("seq", None),
            P(None, "seq", "tp"),
            P("seq", "tp"),
            P("seq", "tp", None),
            P("tp", "seq"),
        ),
        check_vma=False,
    )
```

profile of v0, /device:TPU:1, one launch (start us, length us, event | category | flops | bytes accessed | tf_op | source)
XLA Modules:
  0.0 1995.5 jit_solution(10873285226486419702)
XLA Ops:
  9.0 1.8 multiply_reduce_fusion.3
  11.1 4.4 collective-permute-start
  17.3 2.6 collective-permute-done.1
  21.4 4.1 all_gather.24
  29.1 2.6 all-gather
  32.6 2.6 convolution_convert_fusion.1
  37.9 1.8 convolution_convert_fusion.2
  41.9 126.1 %all-gather.3.cloned.1.call-done = bf16[6144,256]{1,0:T(8,128)(2,1)} async-done(((bf16[192,256]{1,0:T(8,128)(2,1)}), bf16[6144,256]{1,0:T(8,128)(2,1)}) %all-gather.3.cloned.1.call-update) | async-done | bytes 3145744 | tf_op jit(solution)/shard_map/all_gather | solution.py:159
  167.9 79.7 %while.28 = (s32[]{:T(128)}, f32[192,1,6]{0,2,1:T(8,128)S(1)}, f32[192,1,6]{0,2,1:T(8,128)S(1)}, f32[192,1,6,128]{3,0,2,1:T(8,128)S(1)}, bf16[12,512,256]{2,1,0:...) while((s32[]{:T(128)}, f32[192,1,6]{0,2,1:T(8,128)S(1)}, ...), condition=%wide.region_5.6_spmd.clone, body=%wide.region_2.5_spmd.clone.sunk | while | flops 308141504 | bytes 10212029 | solution.py:167
  171.6 1.3 fusion.127
  184.9 1.3 fusion.127
  198.2 1.3 fusion.127
  249.0 2.9 multiply_reduce_fusion.1
  252.9 114.4 %while.29 = (s32[]{:T(128)}, f32[192,1,6,128]{3,0,2,1:T(8,128)}, bf16[12,512,1,256]{3,1,0,2:T(8,128)(2,1)}, bf16[12,512,256]{2,1,0:T(8,128)(2,1)}, bf16[192,1,6,...) while((s32[]{:T(128)}, f32[192,1,6,128]{3,0,2,1:T(8,128)}, ...), condition=%wide.region_9.10_spmd.clone, body=%wide.region_8.9_spmd.clone.sunk | while | flops 762086080 | bytes 16533711 | solution.py:222
  256.6 1.4 fusion.138
  265.2 1.4 fusion.138
  267.9 2.4 fusion.140
  274.8 1.4 fusion.138
  277.5 2.4 fusion.140
  284.4 1.4 fusion.138
  287.1 2.4 fusion.140
  294.0 1.4 fusion.138
  296.7 2.4 fusion.140
  303.6 1.4 fusion.138
  306.3 2.4 fusion.140
  313.3 1.4 fusion.138
  316.0 2.4 fusion.140
  322.9 1.4 fusion.138
  325.6 2.4 fusion.140
  332.5 1.4 fusion.138
  335.2 2.4 fusion.140
  342.2 1.4 fusion.138
  344.9 2.4 fusion.140
  351.8 1.4 fusion.138
  354.5 2.4 fusion.140
  361.4 1.4 fusion.138
  364.1 2.4 fusion.140
  370.6 158.8 %reduce-scatter.9.cloned.1.call-done = bf16[192,256]{1,0:T(8,128)(2,1)} async-done(((bf16[6144,256]{1,0:T(8,128)(2,1)}), bf16[192,256]{1,0:T(8,128)(2,1)}) %reduce-scatter.9.cloned.1.call-update) | async-done | bytes 98320 | tf_op jit(solution)/shard_map/reduce_scatter | solution.py:225
  529.4 2.4 fusion.28
  531.9 45.1 %all-reduce.8.cloned.1.call-done = bf16[192,1536]{1,0:T(8,128)(2,1)} async-done(((bf16[192,1536]{1,0:T(8,128)(2,1)}), bf16[192,1536]{1,0:T(8,128)(2,1)}) %all-reduce.8.cloned.1.call-update) | async-done | bytes 589840 | tf_op jit(solution)/shard_map/psum | solution.py:238
  577.0 1.5 fusion.84
  578.9 1.4 collective-permute-start.2
  580.3 6.2 fusion.91
  586.5 4.0 collective-permute-start.3
  591.4 2.3 copy.52
  593.7 6.1 fusion.30
  599.8 3.2 convolution_convert_fusion
  604.3 4.9 copy.62
  609.5 21.6 %all-reduce.10.cloned.1.call-done = (bf16[192,768]{1,0:T(8,128)(2,1)}, bf16[192,768]{1,0:T(8,128)(2,1)}) async-done(((bf16[192,768]{1,0:T(8,128)(2,1)}, bf16[192,768]{1,0:T(8,128)(2,1)}), (bf16[192,768]{1,0:T(8,128)(2,1)}, bf16[192,768]{1,0:T(8,128)(2,1)})) %all-reduce.10.cloned.1.call-update) | async-done | bytes 589840 | tf_op jit(solution)/shard_map/psum | solution.py:264
  631.1 1.6 multiply_reduce_fusion.2
  632.7 2.0 convolution_bitcast_fusion.5
  638.4 7.2 reduce-scatter.7.cloned.1.call-done
  645.5 1.7 fusion.56
  647.8 1.6 copy.59
  649.4 13.8 reshape_reshape.6
  664.4 2.5 copy.58
  666.9 13.6 copy.55
  680.5 14.4 reshape.294
  694.9 1260.2 %all-reduce.11 = (bf16[5,768,768]{2,1,0:T(8,128)(2,1)}, bf16[1536,1,256]{2,1,0:T(2,128)(2,1)}) all-reduce(f32[5,768,768]{2,1,0:T(8,128)} %reshape.294, f32[1536,1,256]{2,1,0:T(1,128)S(1)} %bitcast.286), channel_id=6, replica_groups=mesh['dp'=2,'seq'=32,'tp'=2] {'dp','seq'}, use_global_device_ids=true, to_apply=%region_17.18.clone | all-reduce | flops 3342336 | bytes 20054016
  1955.9 4.8 all_gather.30
  1962.4 6.2 all_gather.28
  1970.4 5.0 all_gather.31
  1976.8 4.7 all_gather.27
  1983.1 5.0 all_gather.29
  (416 shorter events, 180.7 us)
Async XLA Ops:
  7.2 30.8 %copy-start = (bf16[1536,768]{1,0:T(8,128)(2,1)S(1)}, bf16[1536,768]{1,0:T(8,128)(2,1)}, u32[]{:S(2)}) copy-start(bf16[1536,768]{1,0:T(8,128)(2,1)} %param.17) | copy-start | bytes 7077892
  7.2 160.7 %all-gather.3.cloned.1.call-start = ((), (), s32[]{:S(2)}) async-start(), calls=%async_computation.5 | async-start | bytes 3244032 | tf_op jit(solution)/shard_map/all_gather | solution.py:159
  8.9 11.2 copy-start.27
  9.0 1.8 copy-start.20
  10.8 9.2 copy-start.5
  10.8 9.2 copy-start.25
  11.1 5.7 collective-permute-start
  15.5 4.3 collective-permute-start.1
  20.0 1.4 copy-start.10
  20.1 6.9 copy-start.19
  21.4 4.1 copy-start.13
  21.4 6.7 copy-start.15
  25.5 0.9 copy-start.3
  26.4 0.6 copy-start.23
  28.0 501.4 %reduce-scatter.9.cloned.1.call-start = ((), (), s32[]{:S(2)}) async-start(), calls=%async_computation.7 | async-start | bytes 3244032 | tf_op jit(solution)/shard_map/reduce_scatter | solution.py:225
  31.7 1.0 copy-start.17
  367.3 209.6 %all-reduce.8.cloned.1.call-start = ((), (), s32[]{:S(2)}) async-start(), calls=%async_computation.8 | async-start | bytes 1179648 | tf_op jit(solution)/shard_map/psum | solution.py:238
  368.9 0.7 copy-start.8
  370.6 206.4 %copy-start.4 = (bf16[192,1536]{1,0:T(8,128)(2,1)S(1)}, bf16[192,1536]{1,0:T(8,128)(2,1)}, u32[]{:S(2)}) copy-start(bf16[192,1536]{1,0:T(8,128)(2,1)} %copy-done.3) | copy-start | bytes 1769476
  370.6 206.4 %copy-start.24 = (f32[192]{0:T(256)S(1)}, f32[192]{0:T(256)}, u32[]{:S(2)}) copy-start(f32[192]{0:T(256)} %copy-done.23) | copy-start | bytes 2308
  531.9 46.8 %copy-start.16 = (bf16[1,192,768]{2,1,0:T(8,128)(2,1)S(1)}, bf16[1,192,768]{2,1,0:T(8,128)(2,1)}, u32[]{:S(2)}) copy-start(bf16[1,192,768]{2,1,0:T(8,128)(2,1)} %param.21) | copy-start | bytes 884740
  577.0 1.5 copy-start.12
  578.5 1.8 copy-start.11
  578.9 12.4 copy-start.2
  578.9 11.6 collective-permute-start.2
  586.5 44.6 %all-reduce.10.cloned.1.call-start = ((), (), s32[]{:S(2)}) async-start(), calls=%async_computation.12 | async-start | bytes 1179648 | tf_op jit(solution)/shard_map/psum | solution.py:264
  586.5 4.7 collective-permute-start.3
  593.7 6.2 copy-start.7
  599.8 45.8 %reduce-scatter.7.cloned.1.call-start = ((), (), s32[]{:S(2)}) async-start(), calls=%async_computation.6 | async-start | bytes 884736 | tf_op jit(solution)/shard_map/reduce_scatter | solution.py:174
  599.8 3.7 copy-start.18
  603.1 1366.4 %reduce-scatter.15.cloned.1.call-start = ((), (), s32[]{:S(2)}) async-start(), calls=%async_computation.11 | async-start | bytes 4792320 | tf_op jit(solution)/shard_map/reduce_scatter | solution.py:287
  609.2 21.9 %copy-start.6 = (f32[192,768]{1,0:T(8,128)S(1)}, f32[192,768]{1,0:T(8,128)}, u32[]{:S(2)}) copy-start(f32[192,768]{1,0:T(8,128)} %copy-done.5) | copy-start | bytes 1769476
  609.2 21.9 %copy-start.26 = (f32[192]{0:T(256)S(1)}, f32[192]{0:T(256)}, u32[]{:S(2)}) copy-start(f32[192]{0:T(256)} %copy-done.25) | copy-start | bytes 2308
  609.2 23.4 %copy-start.21 = (pred[192,512]{0,1:T(8,128)(4,1)S(1)}, pred[192,512]{0,1:T(8,128)(4,1)}, u32[]{:S(2)}) copy-start(pred[192,512]{0,1:T(8,128)(4,1)} %copy-done.20) | copy-start | bytes 294916
  609.2 1366.8 %reduce-scatter.11.cloned.1.call-start = ((), (), s32[]{:S(2)}) async-start(), calls=%async_computation.9 | async-start | bytes 1597440 | tf_op jit(solution)/shard_map/reduce_scatter | solution.py:283
  634.7 1.4 copy-start.28
  634.7 3.3 copy-start.9
  634.7 10.8 copy-start.14
  636.0 11.3 copy-start.22
  636.1 1346.1 %reduce-scatter.13.cloned.1.call-start = ((), (), s32[]{:S(2)}) async-start(), calls=%async_computation.10 | async-start | bytes 4792320 | tf_op jit(solution)/shard_map/reduce_scatter | solution.py:285
  1960.7 28.0 %copy-start.1 = (bf16[1536,768]{1,0:T(8,128)(2,1)S(1)}, bf16[1536,768]{1,0:T(8,128)(2,1)}, u32[]{:S(2)}) copy-start(bf16[1536,768]{1,0:T(8,128)(2,1)} %param.17) | copy-start | bytes 7077892
Sparse Core Ops, SparseCore 0:
  28.1 139.7 all-gather.2
  367.5 161.8 reduce-scatter.8
  532.0 44.9 all-reduce.7
  599.9 31.1 all-reduce.9
  633.4 12.0 reduce-scatter.6
  647.8 319.6 reduce-scatter.14
  969.9 349.6 reduce-scatter.10
  1322.1 362.6 reduce-scatter.12
where the time goes:
time: 2010 us; the launch traced here: 2000 us
  blocking collectives  1290 us (64%)
  waiting for transfers between devices  362 us (18%)
  local copies, waits for them, and re-layouts  134 us (7%)
  matrix products  116 us (6%)
  other arithmetic  62.4 us (3%)
    unnamed x1, blocking collectives  1260 us
    reduce_scatter x1, waiting for transfers between devices, per_device(): lax.psum_scatter(pair_partial.astype(jnp.bfloat16), 'seq', scatter_dimens...  159 us
    all_gather x1, waiting for transfers between devices, per_device(): key_rows = lax.all_gather(keyvalue, 'seq', axis=0, tiled=True)  126 us
    psum x1, waiting for transfers between devices, per_device(): lax.psum(normed_partial.astype(jnp.bfloat16), 'tp').astype(jnp.float32)  45.1 us
  transfers between devices with their start and end apart: 12, of which 7 were waited for; matrix products, arithmetic and copies ran while one was open for 5% of the time, Pallas kernels for 0%

commit v1 on v0

v1 whole, which is shorter than its diff:
```python
import functools
import math

import jax
import jax.numpy as jnp
import numpy as np
from jax import lax
from jax.experimental import pallas as pl
from jax.experimental.pallas import tpu as pltpu
from jax.sharding import PartitionSpec as P

ROOT_TWO_PI = math.sqrt(2.0 / math.pi)
CUBIC = 0.044715
EPSILON = 1e-06
DISTANCE_SCALE = 128.0
MESH = pl.DeviceIdType.MESH
LOG2E = math.log2(math.e)
VMEM_LIMIT = 60 * 1024 * 1024

TOK = 192
HEAD = 128
MEMBERS = 6
QW = MEMBERS * HEAD
SCORE_SCALE = LOG2E / math.sqrt(HEAD)
BIAS_SCALE = LOG2E / DISTANCE_SCALE

KV_PARTS = 4
KV_ROWS = TOK // KV_PARTS


def flip(value, low, high):
    value = value + low * (1 - 2 * (value % 2))
    return value + high * (3 - 2 * value)


def seq_peer(seq, moves):
    y, x, z = seq // 8, (seq // 2) % 4, seq % 2
    y = flip(y, moves[2], moves[3])
    x = flip(x, moves[0], moves[1])
    z = z + moves[4] * (1 - 2 * z)
    return (y * 4 + x) * 2 + z


def one_move(seq, direction):
    return seq_peer(seq, [1 if d == direction else 0 for d in range(5)])


def kv_mask(part, place, z):
    bits = [(place >> ((d - part) % 4)) & 1 for d in range(4)]
    x = bits[0] ^ (3 * bits[1])
    y = bits[2] ^ (3 * bits[3])
    return (y << 3) | (x << 1) | z


KV_MASKS = np.array(
    [[[kv_mask(q, p, z) for z in range(2)] for q in range(KV_PARTS)] for p in range(16)], np.int32
)


def enter(peers):
    barrier = pltpu.get_barrier_semaphore()
    for peer in peers:
        pl.semaphore_signal(barrier, inc=1, device_id=peer, device_id_type=MESH)
    pl.semaphore_wait(barrier, len(peers))


def send(src, dst, send_sem, recv_sem, peer):
    return pltpu.make_async_remote_copy(
        src_ref=src,
        dst_ref=dst,
        send_sem=send_sem,
        recv_sem=recv_sem,
        device_id=peer,
        device_id_type=MESH,
    )


NT = (((1,), (1,)), ((), ()))
TN = (((0,), (0,)), ((), ()))


def dot_nt(a, b):
    return lax.dot_general(a, b, NT, preferred_element_type=jnp.float32)


def dot_tn(a, b):
    return lax.dot_general(a, b, TN, preferred_element_type=jnp.float32)


def dot_nn(a, b):
    return jnp.dot(a, b, preferred_element_type=jnp.float32)


def forward_kernel(
    slope_ref, q_ref, kv_ref, back_ref, qpos_ref, kpos_ref,
    att_ref, stat_ref, held_ref,
    acc_ref, top_ref, send_sem, recv_sem, zsend_sem, zrecv_sem,
):
    seq = lax.axis_index("seq")
    peers = [{"seq": one_move(seq, d)} for d in range(5)]
    enter(peers)
    zcopies = []
    for part in range(KV_PARTS):
        rows = pl.ds(part * KV_ROWS, KV_ROWS)
        copy = send(
            kv_ref.at[rows],
            held_ref.at[0, part, pl.ds(KV_ROWS, KV_ROWS)],
            zsend_sem.at[part],
            zrecv_sem.at[part],
            peers[4],
        )
        copy.start()
        zcopies.append(copy)
    for part in range(KV_PARTS):
        held_ref[0, part, 0:KV_ROWS] = kv_ref[part * KV_ROWS : (part + 1) * KV_ROWS]
    acc_ref[...] = jnp.zeros_like(acc_ref)
    top_ref[...] = jnp.full_like(top_ref, -1e30)
    qpos = qpos_ref[...]

    def absorb(pair, kpos):
        keys = pair[:, :HEAD]
        values = jnp.concatenate([pair[:, HEAD:], jnp.ones_like(keys)], axis=1)
        distance = jnp.abs(qpos - kpos)
        for head in range(MEMBERS):
            scores = dot_nt(q_ref[:, head * HEAD : (head + 1) * HEAD], keys) * SCORE_SCALE
            scores = scores - distance * (slope_ref[head] * BIAS_SCALE)
            old = top_ref[head]
            new = jnp.maximum(old, jnp.max(scores, axis=1, keepdims=True))
            fading = jnp.exp2(old - new)
            weights = jnp.exp2(scores - new[:, :1]).astype(jnp.bfloat16)
            acc_ref[head] = acc_ref[head] * jnp.concatenate([fading, fading], axis=1) + dot_nn(
                weights, values
            )
            top_ref[head] = new

    def places(first, count):
        pair = held_ref[pl.ds(first, count)].reshape(count * 2 * TOK, 2 * HEAD)
        if count == 1:
            kpos = kpos_ref[first]
        else:
            kpos = jnp.concatenate([kpos_ref[first + i] for i in range(count)], axis=1)
        absorb(pair, kpos)

    def start_stage(k):
        copies = []
        for part in range(KV_PARTS):
            copy = send(
                held_ref.at[pl.ds(0, 2**k), part],
                held_ref.at[pl.ds(2**k, 2**k), part],
                send_sem.at[k, part],
                recv_sem.at[k, part],
                peers[(part + k) % 4],
            )
            copy.start()
            copies.append(copy)
        return copies

    for copy in zcopies:
        copy.wait()
    stage = start_stage(0)
    places(0, 1)
    for copy in stage:
        copy.wait()
    stage = start_stage(1)
    places(1, 1)
    for copy in stage:
        copy.wait()
    stage = start_stage(2)
    places(2, 2)
    for copy in stage:
        copy.wait()
    stage = start_stage(3)

    def two_places(first):
        def step(i, carry):
            places(first + 2 * i, 2)
            return carry

        return step

    lax.fori_loop(0, 2, two_places(4), 0)
    for copy in stage:
        copy.wait()
    lax.fori_loop(0, 4, two_places(8), 0)
    lane = lax.broadcasted_iota(jnp.int32, (TOK, HEAD), 1)
    stats = jnp.zeros((TOK, HEAD), jnp.float32)
    for head in range(MEMBERS):
        totals = acc_ref[head, :, HEAD:]
        mixed = (acc_ref[head, :, :HEAD] / totals).astype(jnp.bfloat16)
        att_ref[:, head * HEAD : (head + 1) * HEAD] = mixed
        back = back_ref[:, head * HEAD : (head + 1) * HEAD].astype(jnp.float32)
        delta = jnp.sum(back * mixed.astype(jnp.float32), axis=1, keepdims=True)
        stats = jnp.where(lane == head, top_ref[head] + jnp.log2(totals), stats)
        stats = jnp.where(lane == 8 + head, delta, stats)
    stat_ref[...] = stats


def forward_attention(slopes, queries, keyvalue, back_attended, qpos, kpos):
    vmem = pl.BlockSpec(memory_space=pltpu.VMEM)
    return pl.pallas_call(
        forward_kernel,
        out_shape=(
            jax.ShapeDtypeStruct((TOK, QW), jnp.bfloat16),
            jax.ShapeDtypeStruct((TOK, HEAD), jnp.float32),
            jax.ShapeDtypeStruct((16, KV_PARTS, 2 * KV_ROWS, 2 * HEAD), jnp.bfloat16),
        ),
        in_specs=[pl.BlockSpec(memory_space=pltpu.SMEM)] + [vmem] * 5,
        out_specs=(vmem, vmem, vmem),
        scratch_shapes=[
            pltpu.VMEM((MEMBERS, TOK, 2 * HEAD), jnp.float32),
            pltpu.VMEM((MEMBERS, TOK, HEAD), jnp.float32),
            pltpu.SemaphoreType.DMA((4, KV_PARTS)),
            pltpu.SemaphoreType.DMA((4, KV_PARTS)),
            pltpu.SemaphoreType.DMA((KV_PARTS,)),
            pltpu.SemaphoreType.DMA((KV_PARTS,)),
        ],
        compiler_params=pltpu.CompilerParams(
            collective_id=0, has_side_effects=True, vmem_limit_bytes=VMEM_LIMIT
        ),
    )(slopes, queries, keyvalue, back_attended, qpos, kpos)


def backward_kernel(
    kbase_ref, q_ref, back_ref, held_ref, qpos_ref, slope_ref, lse_ref, delta_ref,
    dq_ref, dkv_ref,
    qs_ref, bs_ref, dq_acc, part_ref, land3, land2, land1, land0, landz,
    send_sem, recv_sem, zsend_sem, zrecv_sem,
):
    seq = lax.axis_index("seq")
    peers = [{"seq": one_move(seq, d)} for d in range(5)]
    enter(peers)
    lands = [land0, land1, land2, land3]
    for head in range(MEMBERS):
        rows = slice(head * TOK, (head + 1) * TOK)
        qs_ref[rows] = q_ref[:, head * HEAD : (head + 1) * HEAD]
        bs_ref[rows] = back_ref[:, head * HEAD : (head + 1) * HEAD]
    dq_acc[...] = jnp.zeros_like(dq_acc)
    qpos = qpos_ref[...]
    row = lax.broadcasted_iota(jnp.int32, (KV_ROWS, 1), 0).astype(jnp.float32)

    def one_place(place, carry):
        pair = held_ref[place].reshape(2 * TOK, 2 * HEAD)
        keys, values = pair[:, :HEAD], pair[:, HEAD:]
        kpos = jnp.concatenate([row + kbase_ref[place, g] for g in range(8)], axis=0)
        distance = jnp.abs(qpos - kpos)
        key_grad = jnp.zeros((2 * TOK, HEAD), jnp.float32)
        value_grad = jnp.zeros((2 * TOK, HEAD), jnp.float32)
        for duo in range(MEMBERS // 2):
            rows = slice(duo * 2 * TOK, (duo + 1) * 2 * TOK)
            qd, bd = qs_ref[rows], bs_ref[rows]
            scores = dot_nt(keys, qd) * SCORE_SCALE - distance * slope_ref[duo]
            probs = jnp.exp2(scores - lse_ref[duo])
            back_probs = dot_nt(values, bd)
            grad_scores = (probs * (back_probs - delta_ref[duo])).astype(jnp.bfloat16)
            value_grad = value_grad + dot_nn(probs.astype(jnp.bfloat16), bd)
            key_grad = key_grad + dot_nn(grad_scores, qd)
            dq_acc[rows] += dot_tn(grad_scores, keys)
        both = jnp.concatenate([key_grad * (1.0 / math.sqrt(HEAD)), value_grad], axis=1)
        part_ref[place] = both.astype(jnp.bfloat16).reshape(KV_PARTS, 2 * KV_ROWS, 2 * HEAD)
        return carry

    def start_stage(k):
        copies = []
        for part in range(KV_PARTS):
            copy = send(
                part_ref.at[pl.ds(2**k, 2**k), part],
                lands[k].at[pl.ds(0, 2**k), part],
                send_sem.at[k, part],
                recv_sem.at[k, part],
                peers[(part + k) % 4],
            )
            copy.start()
            copies.append(copy)
        return copies

    def finish_stage(k, copies):
        for copy in copies:
            copy.wait()

        def add(p, carry):
            part_ref[p] = part_ref[p] + lands[k][p]
            return carry

        lax.fori_loop(0, 2**k, add, 0)

    lax.fori_loop(8, 16, one_place, 0)
    copies = start_stage(3)
    lax.fori_loop(0, 8, one_place, 0)
    finish_stage(3, copies)
    for k in (2, 1, 0):
        finish_stage(k, start_stage(k))
    zcopies = []
    for part in range(KV_PARTS):
        copy = send(
            part_ref.at[0, part, pl.ds(KV_ROWS, KV_ROWS)],
            landz.at[part],
            zsend_sem.at[part],
            zrecv_sem.at[part],
            peers[4],
        )
        copy.start()
        zcopies.append(copy)
    for head in range(MEMBERS):
        grad = dq_acc[head * TOK : (head + 1) * TOK] * (1.0 / math.sqrt(HEAD))
        dq_ref[:, head * HEAD : (head + 1) * HEAD] = grad.astype(jnp.bfloat16)
    for part in range(KV_PARTS):
        zcopies[part].wait()
        dkv_ref[part * KV_ROWS : (part + 1) * KV_ROWS] = part_ref[0, part, 0:KV_ROWS] + landz[part]


def backward_attention(kbase, queries, back_attended, held, qpos, slopes, lse, delta):
    vmem = pl.BlockSpec(memory_space=pltpu.VMEM)
    block = (KV_PARTS, 2 * KV_ROWS, 2 * HEAD)
    return pl.pallas_call(
        backward_kernel,
        out_shape=(
            jax.ShapeDtypeStruct((TOK, QW), jnp.bfloat16),
            jax.ShapeDtypeStruct((TOK, 2 * HEAD), jnp.bfloat16),
        ),
        in_specs=[pl.BlockSpec(memory_space=pltpu.SMEM)] + [vmem] * 7,
        out_specs=(vmem, vmem),
        scratch_shapes=[
            pltpu.VMEM((MEMBERS * TOK, HEAD), jnp.bfloat16),
            pltpu.VMEM((MEMBERS * TOK, HEAD), jnp.bfloat16),
            pltpu.VMEM((MEMBERS * TOK, HEAD), jnp.float32),
            pltpu.VMEM((16,) + block, jnp.bfloat16),
            pltpu.VMEM((8,) + block, jnp.bfloat16),
            pltpu.VMEM((4,) + block, jnp.bfloat16),
            pltpu.VMEM((2,) + block, jnp.bfloat16),
            pltpu.VMEM((1,) + block, jnp.bfloat16),
            pltpu.VMEM((KV_PARTS, KV_ROWS, 2 * HEAD), jnp.bfloat16),
            pltpu.SemaphoreType.DMA((4, KV_PARTS)),
            pltpu.SemaphoreType.DMA((4, KV_PARTS)),
            pltpu.SemaphoreType.DMA((KV_PARTS,)),
            pltpu.SemaphoreType.DMA((KV_PARTS,)),
        ],
        compiler_params=pltpu.CompilerParams(
            collective_id=1, has_side_effects=True, vmem_limit_bytes=VMEM_LIMIT
        ),
    )(kbase, queries, back_attended, held, qpos, slopes, lse, delta)


PARTS = 5
CH = 48


def weights_kernel(
    normed_ref, cot_ref, win_ref, last_ref, patch_ref,
    dq_ref, att_ref, conv_ref, pair_ref, emb_ref,
    out_ref, other_ref,
    sums, land4, land3, land2, land1, land0, land_dp, land_tp, land_diag,
    send_sem, recv_sem, fsend_sem, frecv_sem,
    *, factor,
):
    seq, dp, tp = lax.axis_index("seq"), lax.axis_index("dp"), lax.axis_index("tp")
    peers = [{"seq": one_move(seq, d)} for d in range(5)]
    over = {"dp": 1 - dp}
    side = {"tp": 1 - tp}
    diagonal = {"dp": 1 - dp, "tp": 1 - tp}
    enter(peers + [over, side, diagonal])
    lands = [land0, land1, land2, land3, land4]
    first = lax.broadcasted_iota(jnp.int32, (4 * CH, QW // 2), 0) % CH < CH // 2

    def fill(part):
        def step(i, carry):
            group = 7 - i
            where = []
            for j in range(4):
                place = group * 4 + j
                bits = [(place // 2 ** ((d - part) % 5)) % 2 for d in range(5)]
                where.append(seq_peer(seq, bits))

            def rows(ref, start, count):
                return jnp.concatenate([ref[w, start : start + count] for w in where], axis=0)

            if part == 0:
                grads = dot_nn(rows(normed_ref, 0, CH), dq_ref[...])
            elif part == 1:
                grads = dot_nn(rows(cot_ref, 0, CH), att_ref[...])
            elif part < 4:
                grads = dot_nn(rows(win_ref, (part - 2) * CH, CH), conv_ref[...])
            else:
                wide = dot_nn(rows(last_ref, 0, CH), conv_ref[...])
                conv = jnp.where(first, wide[:, : QW // 2], wide[:, QW // 2 :])
                pair = dot_nn(rows(normed_ref, 0, CH), pair_ref[...])
                emb = dot_nn(rows(patch_ref, 0, 16), emb_ref[...])
                emb = jnp.concatenate(
                    [
                        emb[16 * j : 16 * j + 16, 128 * c : 128 * c + 128]
                        for j in range(4)
                        for c in range(3)
                    ],
                    axis=0,
                )
                grads = jnp.concatenate([conv, pair, emb], axis=1)
            sums[part, pl.ds(group * 4, 4)] = grads.astype(jnp.bfloat16).reshape(4, CH, QW)
            return carry

        return step

    def start(part, k):
        copies = []
        if k > 0:
            spans = ((2 ** (k - 1), 2 ** (k - 1)), (0, 2 ** (k - 1)))
        else:
            spans = ((0, 1),)
        for piece, (low, count) in enumerate(spans):
            copy = send(
                sums.at[part, pl.ds(2**k + low, count)],
                lands[k].at[part, pl.ds(low, count)],
                send_sem.at[part, k, piece],
                recv_sem.at[part, k, piece],
                peers[(part + k) % 5],
            )
            copy.start()
            copies.append((copy, low, count))
        return copies

    def settle(part, k, item):
        copy, low, count = item
        copy.wait()

        def add(i, carry):
            sums[part, low + i] = sums[part, low + i] + lands[k][part, low + i]
            return carry

        lax.fori_loop(0, count, add, 0)

    flights = []
    for part in range(PARTS):
        lax.fori_loop(0, 4, fill(part), 0)
        flights.append(start(part, 4))
    for part in range(PARTS):
        lax.fori_loop(4, 8, fill(part), 0)
    for k in (4, 3, 2, 1):
        after = []
        for part in range(PARTS):
            settle(part, k, flights[part][0])
            after.append(start(part, k - 1))
        for part in range(PARTS):
            settle(part, k, flights[part][1])
        flights = after
    finals = []
    for part in range(PARTS):
        settle(part, 0, flights[part][0])
        copy = send(
            sums.at[part, 0], land_dp.at[part], fsend_sem.at[part], frecv_sem.at[part], over
        )
        copy.start()
        finals.append(copy)
    emb_part = sums.at[4, 0, :, pl.ds(640, 128)]
    sidecopy = send(emb_part, land_tp, fsend_sem.at[5], frecv_sem.at[5], side)
    sidecopy.start()
    diagcopy = send(emb_part, land_diag, fsend_sem.at[6], frecv_sem.at[6], diagonal)
    diagcopy.start()
    for part in range(PARTS):
        finals[part].wait()
        total = sums[part, 0].astype(jnp.float32) + land_dp[part].astype(jnp.float32)
        out_ref[part] = total * factor
    sidecopy.wait()
    diagcopy.wait()
    total = land_tp[...].astype(jnp.float32) + land_diag[...].astype(jnp.float32)
    other_ref[...] = total * factor


def weight_gradients(factor, *operands):
    vmem = pl.BlockSpec(memory_space=pltpu.VMEM)
    return pl.pallas_call(
        functools.partial(weights_kernel, factor=factor),
        out_shape=(
            jax.ShapeDtypeStruct((PARTS, CH, QW), jnp.float32),
            jax.ShapeDtypeStruct((CH, HEAD), jnp.float32),
        ),
        in_specs=[vmem] * 10,
        out_specs=(vmem, vmem),
        scratch_shapes=[pltpu.VMEM((PARTS, 32, CH, QW), jnp.bfloat16)]
        + [pltpu.VMEM((PARTS, 2**k, CH, QW), jnp.bfloat16) for k in (4, 3, 2, 1, 0)]
        + [
            pltpu.VMEM((PARTS, CH, QW), jnp.bfloat16),
            pltpu.VMEM((CH, HEAD), jnp.bfloat16),
            pltpu.VMEM((CH, HEAD), jnp.bfloat16),
            pltpu.SemaphoreType.DMA((PARTS, 5, 2)),
            pltpu.SemaphoreType.DMA((PARTS, 5, 2)),
            pltpu.SemaphoreType.DMA((7,)),
            pltpu.SemaphoreType.DMA((7,)),
        ],
        compiler_params=pltpu.CompilerParams(
            collective_id=2, has_side_effects=True, vmem_limit_bytes=VMEM_LIMIT
        ),
    )(*operands)


def gelu_value(inputs):
    return (
        0.5 * inputs * (1.0 + jnp.tanh(ROOT_TWO_PI * (inputs + CUBIC * inputs * inputs * inputs)))
    )


def gelu_slope(inputs):
    inner = jnp.tanh(ROOT_TWO_PI * (inputs + CUBIC * inputs * inputs * inputs))
    return 0.5 * (1.0 + inner) + 0.5 * inputs * (1.0 - inner * inner) * ROOT_TWO_PI * (
        1.0 + 3.0 * CUBIC * inputs * inputs
    )


def inverse_rms(values):
    return lax.rsqrt(jnp.mean(values * values, axis=-1, keepdims=True) + EPSILON)


def unpack_local(packed, bases_tok):
    shift_bits = 2 * jnp.arange(16, dtype=jnp.int32)
    fields = jnp.right_shift(packed[:, None], shift_bits) & 3
    letters = fields.reshape(-1, bases_tok)
    onehot = letters[..., None] == jnp.arange(4, dtype=jnp.int32)
    return onehot.reshape(letters.shape[0], 4 * bases_tok).astype(jnp.bfloat16)


def sequence_rims(shard, width):
    size, length = lax.axis_size("seq"), shard.shape[0]
    up = [(i, (i + 1) % size) for i in range(size - 1)]
    down = [(j, i) for i, j in up]
    before = lax.ppermute(shard[length - width :], "seq", up)
    after = lax.ppermute(shard[:width], "seq", down)
    return jnp.concatenate([before, shard, after], axis=0)


def feature_halves(values):
    return lax.all_gather(values, "tp", axis=1, tiled=True)


def from_side(values):
    return lax.ppermute(values, "tp", [(0, 1), (1, 0)])


def per_device(
    bases,
    shifts,
    embed_weight,
    conv_weight,
    query_weight,
    keyvalue_weight,
    output_weight,
    slopes,
    cotangent,
):
    tokens = cotangent.shape[1]
    conv_in = embed_weight.shape[1]
    bases_tok = embed_weight.shape[0] // 4
    taps_count = conv_weight.shape[0]
    reach_rows = taps_count // 2
    local_out = conv_weight.shape[2]
    width_all = query_weight.shape[0]
    seq, tp = lax.axis_index("seq"), lax.axis_index("tp")
    seq_count = lax.axis_size("seq")

    patches = unpack_local(bases[0], bases_tok)
    embedded = jnp.dot(patches, embed_weight, preferred_element_type=jnp.float32).astype(
        jnp.bfloat16
    )
    embedded_wide = embedded.astype(jnp.float32)
    scale_in = inverse_rms(embedded_wide)
    normed_in = embedded_wide * scale_in
    activated = gelu_value(normed_in).astype(jnp.bfloat16)
    padded = sequence_rims(activated, reach_rows)
    windows = jnp.concatenate(
        [padded[tap_index : tap_index + tokens] for tap_index in range(taps_count)], axis=-1
    )
    convolved = jnp.dot(
        windows,
        conv_weight.reshape(taps_count * conv_in, local_out),
        preferred_element_type=jnp.float32,
    )
    hidden = (convolved + embedded_wide).astype(jnp.bfloat16)
    hidden_full = feature_halves(hidden).astype(jnp.float32)
    scale_mid = inverse_rms(hidden_full)
    normed_wide = hidden_full * scale_mid
    normed = normed_wide.astype(jnp.bfloat16)
    queries = jnp.dot(normed, query_weight, preferred_element_type=jnp.float32).astype(jnp.bfloat16)
    pair_weight = keyvalue_weight.reshape(width_all, 2 * HEAD)
    keyvalue = jnp.dot(normed, pair_weight, preferred_element_type=jnp.float32).astype(jnp.bfloat16)

    cotangent_local = cotangent[0]
    cotangent_full = feature_halves(cotangent_local)
    back_attended = jnp.einsum(
        "tc,qc->tq", cotangent_full, output_weight, preferred_element_type=jnp.float32
    ).astype(jnp.bfloat16)

    token = jnp.arange(tokens, dtype=jnp.int32)
    qpos = (seq * tokens + token + shifts[0]).astype(jnp.float32)
    sources = jnp.bitwise_xor(seq, KV_MASKS) * tokens
    kbase = sources + (KV_ROWS * np.arange(KV_PARTS, dtype=np.int32))[None, :, None]
    kbase = kbase.reshape(16, 2 * KV_PARTS)
    kpos = kbase[:, :, None] + jnp.arange(KV_ROWS, dtype=jnp.int32)
    kpos = kpos.reshape(16, 1, 2 * tokens).astype(jnp.float32)
    attended, stats, held = forward_attention(
        slopes, queries, keyvalue, back_attended, qpos.reshape(tokens, 1), kpos
    )
    lse = stats[:, :MEMBERS].T.reshape(MEMBERS // 2, 1, 2 * tokens)
    delta = stats[:, 8 : 8 + MEMBERS].T.reshape(MEMBERS // 2, 1, 2 * tokens)

    partial_out = jnp.dot(attended, output_weight, preferred_element_type=jnp.float32).astype(
        jnp.bfloat16
    )
    halves = partial_out.reshape(tokens, 2, local_out)
    mine = jnp.where(tp == 0, halves[:, 0], halves[:, 1])
    yours = jnp.where(tp == 0, halves[:, 1], halves[:, 0])
    projected = mine.astype(jnp.float32) + from_side(yours).astype(jnp.float32)
    result = (hidden.astype(jnp.float32) + projected).astype(jnp.bfloat16)

    slope_rows = jnp.repeat(slopes * BIAS_SCALE, tokens).reshape(MEMBERS // 2, 1, 2 * tokens)
    back_query, back_pair = backward_attention(
        kbase.astype(jnp.float32),
        queries,
        back_attended,
        held,
        jnp.tile(qpos, 2).reshape(1, 2 * tokens),
        slope_rows,
        lse,
        delta,
    )

    normed_partial = jnp.einsum(
        "tq,cq->tc", back_query, query_weight, preferred_element_type=jnp.float32
    )
    normed_partial = normed_partial + jnp.einsum(
        "tq,cq->tc", back_pair, pair_weight, preferred_element_type=jnp.float32
    )
    normed_partial = normed_partial.astype(jnp.bfloat16)
    back_normed = normed_partial.astype(jnp.float32) + from_side(normed_partial).astype(jnp.float32)
    back_wide = scale_mid * (
        back_normed - normed_wide * jnp.mean(back_normed * normed_wide, axis=-1, keepdims=True)
    )
    back_hidden = cotangent_local.astype(jnp.float32) + lax.dynamic_slice_in_dim(
        back_wide, tp * local_out, local_out, 1
    )
    back_conv = back_hidden.astype(jnp.bfloat16)
    back_padded = sequence_rims(back_conv, reach_rows)
    back_windows = jnp.concatenate(
        [
            back_padded[taps_count - 1 - tap_index : taps_count - 1 - tap_index + tokens]
            for tap_index in range(taps_count)
        ],
        axis=-1,
    )
    active_partial = jnp.einsum(
        "tko,kco->tc",
        back_windows.reshape(tokens, taps_count, local_out),
        conv_weight,
        preferred_element_type=jnp.float32,
    ).astype(jnp.bfloat16)
    ours = jnp.concatenate([active_partial, back_conv], axis=1)
    summed = ours.astype(jnp.float32) + from_side(ours).astype(jnp.float32)
    back_active, back_residual = summed[:, :conv_in], summed[:, conv_in:]
    back_normed_in = back_active * gelu_slope(normed_in)
    back_embedded = back_residual + scale_in * (
        back_normed_in - normed_in * jnp.mean(back_normed_in * normed_in, axis=-1, keepdims=True)
    )
    back_embedded = back_embedded.astype(jnp.bfloat16)
    half = conv_in // 2
    emb_half = jnp.where(tp == 0, back_embedded[:, :half], back_embedded[:, half:])

    rows = conv_in // seq_count
    by_chunk = windows.reshape(tokens, taps_count, seq_count, rows).transpose(2, 1, 3, 0)
    early = by_chunk[:, :4].reshape(seq_count, 4 * rows, tokens)
    last = jnp.concatenate([by_chunk[:, 4], by_chunk[:, 4]], axis=1)
    factor = (lax.axis_size("dp") * seq_count * tokens) ** (-0.5)
    sums, other = weight_gradients(
        factor,
        normed.T.reshape(seq_count, CH, tokens),
        cotangent_full.T.reshape(seq_count, CH, tokens),
        early,
        last,
        patches.T.reshape(seq_count, 16, tokens),
        back_query,
        attended,
        back_conv,
        back_pair,
        emb_half,
    )
    grad_query = sums[0]
    grad_output = sums[1].T
    tail = sums[4, :, :half]
    tail = jnp.concatenate([tail[:rows], tail[rows:]], axis=1)
    grad_conv = jnp.concatenate([sums[2:4].reshape(4, rows, local_out), tail[None]], axis=0)
    grad_pair = sums[4, :, half : half + 2 * HEAD].reshape(CH, 1, 2 * HEAD)

    def embed_rows(block):
        return jnp.concatenate([block[:16], block[16:32], block[32:]], axis=1)

    own, others = embed_rows(sums[4, :, half + 2 * HEAD :]), embed_rows(other)
    grad_embed = jnp.concatenate(
        [jnp.where(tp == 0, own, others), jnp.where(tp == 0, others, own)], axis=1
    )
    return (result[None], grad_embed, grad_conv, grad_query, grad_pair, grad_output)


def solution(mesh):
    placed = (
        P("dp", "seq"),
        P("dp"),
        P(),
        P(None, None, "tp"),
        P(None, "tp"),
        P(None, "tp", None),
        P("tp", None),
        P("tp"),
        P("dp", "seq", "tp"),
    )
    return jax.shard_map(
        per_device,
        mesh=mesh,
        in_specs=placed,
        out_specs=(
            P("dp", "seq", "tp"),
            P("seq", None),
            P(None, "seq", "tp"),
            P("seq", "tp"),
            P("seq", "tp", None),
            P("tp", "seq"),
        ),
        check_vma=False,
    )
```

time: 2010 us -> 271 us (0.13)
  blocking collectives: 1290 us -> 5.17 us
  waiting for transfers between devices: 362 us -> 0.02 us
  Pallas kernels: 0 us -> 162 us
  local copies, waits for them, and re-layouts: 134 us -> 32.6 us
  matrix products: 116 us -> 23.6 us
  other arithmetic: 62.4 us -> 23.4 us
    unnamed x1 -> x0, blocking collectives: 1260 us -> none
    reduce_scatter x5 -> x0, waiting for transfers between devices: 166 us -> none  [the longest x1 159 us: per_device(): lax.psum_scatter(pair_partial.astype(jnp.bfloat16), 'seq', scatter_dimens...]
    pallas_call x0 -> x3, Pallas kernels: none -> 162 us  [the longest x1 77.6 us: weight_gradients(): pl.pallas_call(functools.partial(weights_kernel, factor=factor), out_shap...]
    all_gather x1 -> x0, waiting for transfers between devices: 126 us -> none  [per_device(): key_rows = lax.all_gather(keyvalue, 'seq', axis=0, tiled=True)]
    dot_general x89 -> x0, matrix products: 94.5 us -> none  [the longest x24 32.8 us: score_block(): jnp.einsum('qgmd,kgd->qgmk', grouped_query, keys_now, preferred_element_t...]
    psum x2 -> x0, waiting for transfers between devices: 66.7 us -> none  [the longest x1 45.1 us: per_device(): lax.psum(normed_partial.astype(jnp.bfloat16), 'tp').astype(jnp.float32)]
    reshape x29 -> x3, local copies, waits for them, and re-layouts: 40.8 us -> 3.34 us  [the longest x1 1.97 us: per_device(): halves = partial_out.reshape(tokens, 2, local_out)]
    dynamic_slice x24 -> x0, local copies, waits for them, and re-layouts: 29.8 us -> none  [per_device(): lax.scan(scan_step, start_state, (blocked, block_firsts))]
  transfers between devices with their start and end apart: 12 -> 7, of which waited for: 7 -> 0; matrix products, arithmetic and copies ran while one was open for 5% -> 17% of each run, Pallas kernels for 0% -> 0%
where the time goes in v1:
time: 271 us; the launch traced here: 269 us
  Pallas kernels  162 us (60%)
  local copies, waits for them, and re-layouts  32.6 us (12%)
  matrix products  23.6 us (9%)
  other arithmetic  23.4 us (9%)
  starting transfers between devices  20.5 us (8%)
  blocking collectives  5.17 us (2%)
    pallas_call x1, Pallas kernels, weight_gradients(): pl.pallas_call(functools.partial(weights_kernel, factor=factor), out_shap...  77.6 us
    pallas_call x1, Pallas kernels, backward_attention(): pl.pallas_call(backward_kernel, out_shape=(jax.ShapeDtypeStruct((TOK, QW)...  43.6 us
    pallas_call x1, Pallas kernels, forward_attention(): pl.pallas_call(forward_kernel, out_shape=(jax.ShapeDtypeStruct((TOK, QW),...  41 us
    ppermute x2, starting transfers between devices, sequence_rims(): before = lax.ppermute(shard[length - width:], 'seq', up)  9.2 us
    ppermute x3, starting transfers between devices, from_side(): return lax.ppermute(values, 'tp', [(0, 1), (1, 0)])  8.77 us
    unnamed x8, other arithmetic  5.79 us
  transfers between devices with their start and end apart: 7, of which 0 were waited for; matrix products, arithmetic and copies ran while one was open for 17% of the time, Pallas kernels for 0%

profile of v1, /device:TPU:1, one launch (start us, length us, event | category | flops | bytes accessed | tf_op | source)
XLA Modules:
  0.0 269.3 jit_solution(2397151820120133200)
XLA Ops:
  0.7 0.9 reduce
  2.3 0.9 fusion.38
  3.2 1.7 multiply_reduce_fusion.2
  5.7 4.9 %collective-permute-start = (bf16[2,768]{1,0:T(2,128)(2,1)}, bf16[2,768]{1,0:T(2,128)(2,1)}, u32[]{:S(2)}, u32[]{:S(2)}) collective-permute-start(bf16[2,768]{1,0:T(2,128)(2,1)} %get-tuple-element.56), channel_id=1, source_target_pairs={{0,2},{2,4},{4,6},{6,8},{8,10},{10,12},{12,14},{14,16},{16,18},{18... | collective-permute-start | bytes 9224 | tf_op jit(solution)/shard_map/ppermute | solution.py:522
  10.7 1.3 collective-permute-start.1
  12.8 0.7 add.151
  13.5 1.6 add.152
  15.2 2.8 %all-gather = bf16[1,192,1536]{2,1,0:T(8,128)(2,1)S(1)} all-gather(bf16[1,192,768]{2,1,0:T(8,128)(2,1)S(1)} %copy-done.13), channel_id=2, replica_groups=mesh['dp'=2,'seq'=32,'tp'=2] {'tp'}, dimensions={2}, use_global_device_ids=true | all-gather | bytes 884736 | tf_op jit(solution)/shard_map/all_gather | solution.py:528
  18.0 0.7 broadcast_multiply_fusion.2
  18.6 0.7 add_convert_fusion.qpos_ref
  19.3 1.4 add_convert_fusion.1.kpos_ref
  20.6 3.3 %convolution_convert_fusion.1.back_ref = bf16[192,768]{1,0:T(8,128)(2,1)} fusion(bf16[768,1536]{1,0:T(8,128)(2,1)} %param.17, bf16[1,192,1536]{2,1,0:T(8,128)(2,1)S(1)} %all-gather), kind=kOutput, calls=%fused_computation.9 | convolution fusion | flops 453132288 | bytes 3244032 | tf_op jit(solution)/shard_map/tc,qc->tq/dot_general | solution.py:584
  24.6 0.7 copy.52.kbase_ref
  25.4 0.7 broadcast_in_dim.23.slope_ref
  26.1 0.7 fusion.27
  26.8 0.8 fusion.32
  27.9 0.7 fusion.25
  28.6 0.7 fusion.31
  29.4 4.6 %fusion.1 = bf16[192,768]{1,0:T(8,128)(2,1)S(1)} fusion(f32[192,768]{1,0:T(8,128)S(1)} %get-tuple-element.65, bf16[192,3840]{1,0:T(8,128)(2,1)S(1)} %fusion.31, bf16[3840,768]{1,0:T(8,128)(2,1)} %bitcast.98), kind=kOutput, calls=%fused_computation.7 | convolution fusion | flops 1132756992 | bytes 8257536 | tf_op jit(solution)/shard_map/dot_general | solution.py:568
  34.0 2.4 all_gather.6
  36.5 1.0 convolution_convert_fusion.4.kv_ref
  37.6 1.4 convolution_convert_fusion.2.q_ref
  39.0 41.0 %shard_map.154 = (bf16[192,768]{1,0:T(8,128)(2,1)}, f32[192,128]{1,0:T(8,128)}, bf16[16,4,96,256]{3,2,1,0:T(8,128)(2,1)}) custom-call(f32[6]{0:T(128)} %slope_ref.1, bf16[192,768]{1,0:T(8,128)(2,1)} %convolution_convert_fusion.2.q_ref, bf16[192,256]{1,0:T(8,128)(2,1)} %convolution_convert_fusion.4.kv_ref, ...), custom_call_target="tpu_custom_call" | custom-call | tf_op jit(solution)/shard_map/pallas_call | solution.py:200
  79.9 1.1 slice_bitcast_fusion.3
  81.1 0.7 reshape.201.lse_ref
  81.8 0.7 reshape.202.delta_ref
  82.5 43.6 %shard_map.155 = (bf16[192,768]{1,0:T(8,128)(2,1)}, bf16[192,256]{1,0:T(8,128)(2,1)}) custom-call(f32[16,8]{1,0:T(8,128)} %copy.52.kbase_ref, bf16[192,768]{1,0:T(8,128)(2,1)} %convolution_convert_fusion.2.q_ref, bf16[192,768]{1,0:T(8,128)(2,1)} %convolution_convert_fusion.1.back_ref, bf16[16,4,96,256]{3,2,1,0:T(8,128)(2,1)} %get-tuple-element.14.held_ref, ...), custom_call_target="tpu_custom_call" | custom-call | tf_op jit(solution)/shard_map/pallas_call | solution.py:314
  126.1 1.9 fusion.43
  128.1 1.2 fusion
  129.3 8.3 %collective-permute-start.3 = (bf16[192,1536]{1,0:T(8,128)(2,1)}, bf16[192,1536]{1,0:T(8,128)(2,1)}, u32[]{:S(2)}, u32[]{:S(2)}) collective-permute-start(bf16[192,1536]{1,0:T(8,128)(2,1)} %fusion), channel_id=1, source_target_pairs={{0,1},{1,0},{2,3},{3,2},{4,5},{5,4},{6,7},{7,6},{8,9},{9,8},{10,11... | collective-permute-start | bytes 1769480 | tf_op jit(solution)/shard_map/ppermute | solution.py:532
  137.6 1.2 copy.47
  138.8 3.2 %convolution_convert_fusion = bf16[192,1536]{1,0:T(8,128)(2,1)} fusion(bf16[192,768]{1,0:T(8,128)(2,1)} %get-tuple-element.13.att_ref, bf16[768,1536]{1,0:T(8,128)(2,1)} %param.17), kind=kOutput, calls=%fused_computation.1 | convolution fusion | flops 453279744 | bytes 3244032 | tf_op jit(solution)/shard_map/dot_general | solution.py:601
  142.0 2.0 reshape.194
  144.0 0.8 fusion.39
  145.0 2.7 multiply_reduce_fusion
  148.0 1.3 collective-permute-start.4
  149.3 0.8 select_bitcast_fusion
  150.1 3.7 %copy.48 = bf16[192,3840]{0,1:T(8,128)(2,1)} copy(bf16[192,3840]{1,0:T(8,128)(2,1)} %copy-done.10) | data formatting | bytes 2949120 | tf_op jit(solution)/shard_map/concatenate | solution.py:565
  153.8 1.5 slice.182
  155.3 1.4 copy.49
  156.7 4.3 %collective-permute-start.5 = (bf16[2,768]{1,0:T(2,128)(2,1)S(1)}, bf16[2,768]{1,0:T(2,128)(2,1)S(1)}, u32[]{:S(2)}, u32[]{:S(2)}) collective-permute-start(bf16[2,768]{1,0:T(2,128)(2,1)S(1)} %get-tuple-element.53), channel_id=1, source_target_pairs={{0,2},{2,4},{4,6},{6,8},{8,10},{10,12},{12,14},{14,16},{16,18},{18... | collective-permute-start | bytes 9224 | tf_op jit(solution)/shard_map/ppermute | solution.py:522
  161.0 0.8 fusion.23
  161.8 0.8 fusion.30
  162.6 0.8 constant_dynamic-update-slice_fusion.1
  163.4 0.8 fusion.21
  164.2 0.8 fusion.29
  165.0 3.7 %copy.53 = bf16[192,3840]{0,1:T(8,128)(2,1)} copy(bf16[192,3840]{1,0:T(8,128)(2,1)} %fusion.29) | data formatting | bytes 2949120 | tf_op jit(solution)/shard_map/concatenate | solution.py:638
  168.7 5.3 %fusion.2 = bf16[192,768]{1,0:T(8,128)(2,1)S(1)} fusion(bf16[192,5,768]{0,2,1:T(8,128)(2,1)} %bitcast.93, bf16[5,768,768]{2,1,0:T(8,128)(2,1)} %param.14), kind=kOutput, calls=%fused_computation.8 | convolution fusion | flops 1132609536 | bytes 7667712 | tf_op jit(solution)/shard_map/tko,kco->tc/dot_general | solution.py:645
  174.1 0.9 pad_maximum_fusion.1
  175.5 1.0 slice_bitcast_fusion
  176.5 1.0 pad_maximum_fusion.last_ref
  177.5 1.8 fusion.28
  179.3 2.2 copy.46
  181.5 1.2 convert_add_fusion
  183.9 0.7 slice_select_fusion.emb_ref
  184.6 77.6 %shard_map.156 = (f32[5,48,768]{2,1,0:T(8,128)}, f32[48,128]{1,0:T(8,128)}) custom-call(bf16[32,48,192]{2,1,0:T(8,128)(2,1)} %bitcast.92, bf16[32,48,192]{2,1,0:T(8,128)(2,1)} %bitcast.91, bf16[32,96,192]{2,1,0:T(8,128)(2,1)} %bitcast.89, bf16[32,48,192]{2,1,0:T(8,128)(2,1)} %pad_maximum_fusion.last_ref, bf16[32,16,192]{2,1,0:T(8,128)(2,1)} %bitcast.95, ...), custom_call_target="tpu_custom_call" | custom-call | tf_op jit(solution)/shard_map/pallas_call | solution.py:468
  262.2 0.8 slice_bitcast_fusion.7
  263.0 1.0 slice.166
  264.0 1.7 slice_bitcast_fusion.1
  265.7 0.7 slice_bitcast_fusion.10
  266.5 0.8 slice_bitcast_fusion.5
  267.3 0.7 copy.55
  267.9 0.8 pad_maximum_fusion.2
  268.7 0.6 pad_maximum_fusion.7
  (87 shorter events, 5.4 us)
Async XLA Ops:
  0.6 36.9 %copy-start = (bf16[1536,768]{1,0:T(8,128)(2,1)S(1)}, bf16[1536,768]{1,0:T(8,128)(2,1)}, u32[]{:S(2)}) copy-start(bf16[1536,768]{1,0:T(8,128)(2,1)} %param.15) | copy-start | bytes 7077892
  2.3 10.3 %copy-start.19 = (s32[16,4,2]{0,2,1:T(2,128)S(1)}, s32[16,4,2]{0,2,1:T(2,128)}, u32[]{:S(2)}) copy-start(s32[16,4,2]{0,2,1:T(2,128)} %constant.49.clone) | copy-start | bytes 1540
  3.2 12.0 %copy-start.13 = (bf16[1,192,768]{2,1,0:T(8,128)(2,1)S(1)}, bf16[1,192,768]{2,1,0:T(8,128)(2,1)}, u32[]{:S(2)}) copy-start(bf16[1,192,768]{2,1,0:T(8,128)(2,1)} %param.19) | copy-start | bytes 884740
  5.7 20.3 %collective-permute-start = (bf16[2,768]{1,0:T(2,128)(2,1)}, bf16[2,768]{1,0:T(2,128)(2,1)}, u32[]{:S(2)}, u32[]{:S(2)}) collective-permute-start(bf16[2,768]{1,0:T(2,128)(2,1)} %get-tuple-element.56), channel_id=1, source_target_pairs={{0,2},{2,4},{4,6},{6,8},{8,10},{10,12},{12,14},{14,16},{16,18},{18... | collective-permute-start | bytes 9224 | tf_op jit(solution)/shard_map/ppermute | solution.py:522
  10.7 17.2 %collective-permute-start.1 = (bf16[2,768]{1,0:T(2,128)(2,1)}, bf16[2,768]{1,0:T(2,128)(2,1)}, u32[]{:S(2)}, u32[]{:S(2)}) collective-permute-start(bf16[2,768]{1,0:T(2,128)(2,1)} %get-tuple-element.55), channel_id=1, source_target_pairs={{2,0},{4,2},{6,4},{8,6},{10,8},{12,10},{14,12},{16,14},{18,16},{20... | collective-permute-start | bytes 9224 | tf_op jit(solution)/shard_map/ppermute | solution.py:523
  18.0 6.0 %copy-start.2 = (bf16[1,192,1536]{2,1,0:T(8,128)(2,1)}, bf16[1,192,1536]{2,1,0:T(8,128)(2,1)S(1)}, u32[]{:S(2)}) copy-start(bf16[1,192,1536]{2,1,0:T(8,128)(2,1)S(1)} %all-gather) | copy-start | bytes 1769476
  29.4 4.6 %copy-start.10 = (bf16[192,3840]{1,0:T(8,128)(2,1)}, bf16[192,3840]{1,0:T(8,128)(2,1)S(1)}, u32[]{:S(2)}) copy-start(bf16[192,3840]{1,0:T(8,128)(2,1)S(1)} %fusion.31) | copy-start | bytes 4423684
  33.9 3.6 %copy-start.11 = (bf16[192,768]{1,0:T(8,128)(2,1)}, bf16[192,768]{1,0:T(8,128)(2,1)S(1)}, u32[]{:S(2)}) copy-start(bf16[192,768]{1,0:T(8,128)(2,1)S(1)} %fusion.1) | copy-start | bytes 884740
  34.0 2.6 copy-start.15
  36.3 1.2 copy-start.8
  126.1 2.0 copy-start.16
  126.1 2.0 copy-start.17
  128.1 9.5 %copy-start.3 = (bf16[1,192,1536]{2,1,0:T(8,128)(2,1)S(1)}, bf16[1,192,1536]{2,1,0:T(8,128)(2,1)}, u32[]{:S(2)}) copy-start(bf16[1,192,1536]{2,1,0:T(8,128)(2,1)} %copy-done.2) | copy-start | bytes 1769476
  129.3 15.5 %collective-permute-start.3 = (bf16[192,1536]{1,0:T(8,128)(2,1)}, bf16[192,1536]{1,0:T(8,128)(2,1)}, u32[]{:S(2)}, u32[]{:S(2)}) collective-permute-start(bf16[192,1536]{1,0:T(8,128)(2,1)} %fusion), channel_id=1, source_target_pairs={{0,1},{1,0},{2,3},{3,2},{4,5},{5,4},{6,7},{7,6},{8,9},{9,8},{10,11... | collective-permute-start | bytes 1769480 | tf_op jit(solution)/shard_map/ppermute | solution.py:532
  144.0 1.1 copy-start.9
  144.8 4.5 %copy-start.4 = (bf16[192,1,768]{2,1,0:T(2,128)(2,1)}, bf16[192,1,768]{2,1,0:T(2,128)(2,1)S(1)}, u32[]{:S(2)}) copy-start(bf16[192,1,768]{2,1,0:T(2,128)(2,1)S(1)} %get-tuple-element.51) | copy-start | bytes 884740
  144.8 4.5 %copy-start.6 = (bf16[192,1,768]{2,1,0:T(2,128)(2,1)}, bf16[192,1,768]{2,1,0:T(2,128)(2,1)S(1)}, u32[]{:S(2)}) copy-start(bf16[192,1,768]{2,1,0:T(2,128)(2,1)S(1)} %get-tuple-element.52) | copy-start | bytes 884740
  144.8 2.9 %copy-start.14 = (bf16[1,192,768]{2,1,0:T(8,128)(2,1)S(1)}, bf16[1,192,768]{2,1,0:T(8,128)(2,1)}, u32[]{:S(2)}) copy-start(bf16[1,192,768]{2,1,0:T(8,128)(2,1)} %param.19) | copy-start | bytes 884740
  147.9 33.6 %copy-start.1 = (bf16[192,768]{1,0:T(8,128)(2,1)}, bf16[192,768]{1,0:T(8,128)(2,1)S(1)}, u32[]{:S(2)}) copy-start(bf16[192,768]{1,0:T(8,128)(2,1)S(1)} %fusion.16.conv_ref) | copy-start | bytes 884740
  148.0 13.0 %collective-permute-start.4 = (bf16[2,768]{1,0:T(2,128)(2,1)S(1)}, bf16[2,768]{1,0:T(2,128)(2,1)S(1)}, u32[]{:S(2)}, u32[]{:S(2)}) collective-permute-start(bf16[2,768]{1,0:T(2,128)(2,1)S(1)} %get-tuple-element.54), channel_id=1, source_target_pairs={{2,0},{4,2},{6,4},{8,6},{10,8},{12,10},{14,12},{16,14},{18,16},{20... | collective-permute-start | bytes 9224 | tf_op jit(solution)/shard_map/ppermute | solution.py:523
  156.7 20.7 %collective-permute-start.2 = (bf16[192,768]{1,0:T(8,128)(2,1)}, bf16[192,768]{1,0:T(8,128)(2,1)}, u32[]{:S(2)}, u32[]{:S(2)}) collective-permute-start(bf16[192,768]{1,0:T(8,128)(2,1)} %select_bitcast_fusion), channel_id=1, source_target_pairs={{0,1},{1,0},{2,3},{3,2},{4,5},{5,4},{6,7},{7,6},{8,9},{9,8},{10,11... | collective-permute-start | bytes 884744 | tf_op jit(solution)/shard_map/ppermute | solution.py:532
  156.7 6.7 %collective-permute-start.5 = (bf16[2,768]{1,0:T(2,128)(2,1)S(1)}, bf16[2,768]{1,0:T(2,128)(2,1)S(1)}, u32[]{:S(2)}, u32[]{:S(2)}) collective-permute-start(bf16[2,768]{1,0:T(2,128)(2,1)S(1)} %get-tuple-element.53), channel_id=1, source_target_pairs={{0,2},{2,4},{4,6},{6,8},{8,10},{10,12},{12,14},{14,16},{16,18},{18... | collective-permute-start | bytes 9224 | tf_op jit(solution)/shard_map/ppermute | solution.py:522
  174.0 3.4 %copy-start.5 = (bf16[192,1,768]{2,1,0:T(2,128)(2,1)S(1)}, bf16[192,1,768]{2,1,0:T(2,128)(2,1)}, u32[]{:S(2)}) copy-start(bf16[192,1,768]{2,1,0:T(2,128)(2,1)} %copy-done.4) | copy-start | bytes 884740
  174.1 3.4 %copy-start.7 = (bf16[192,1,768]{2,1,0:T(2,128)(2,1)S(1)}, bf16[192,1,768]{2,1,0:T(2,128)(2,1)}, u32[]{:S(2)}) copy-start(bf16[192,1,768]{2,1,0:T(2,128)(2,1)} %copy-done.6) | copy-start | bytes 884740
  174.1 3.4 %copy-start.12 = (bf16[192,768]{1,0:T(8,128)(2,1)S(1)}, bf16[192,768]{1,0:T(8,128)(2,1)}, u32[]{:S(2)}) copy-start(bf16[192,768]{1,0:T(8,128)(2,1)} %copy-done.11) | copy-start | bytes 884740
  175.0 6.6 %collective-permute-start.6 = (bf16[192,1536]{1,0:T(8,128)(2,1)}, bf16[192,1536]{1,0:T(8,128)(2,1)}, u32[]{:S(2)}, u32[]{:S(2)}) collective-permute-start(bf16[192,1536]{1,0:T(8,128)(2,1)} %pad_maximum_fusion.1), channel_id=1, source_target_pairs={{0,1},{1,0},{2,3},{3,2},{4,5},{5,4},{6,7},{7,6},{8,9},{9,8},{10,11... | collective-permute-start | bytes 1769480 | tf_op jit(solution)/shard_map/ppermute | solution.py:532
  262.2 5.0 %copy-start.18 = (f32[48,128]{1,0:T(8,128)S(1)}, f32[48,128]{1,0:T(8,128)}, u32[]{:S(2)}) copy-start(f32[48,128]{1,0:T(8,128)} %get-tuple-element.19) | copy-start | bytes 73732

commit v2 on v1

v2 whole, which is shorter than its diff:
```python
import functools
import math

import jax
import jax.numpy as jnp
import numpy as np
from jax import lax
from jax.experimental import pallas as pl
from jax.experimental.pallas import tpu as pltpu
from jax.sharding import PartitionSpec as P

ROOT_TWO_PI = math.sqrt(2.0 / math.pi)
CUBIC = 0.044715
EPSILON = 1e-06
DISTANCE_SCALE = 128.0
MESH = pl.DeviceIdType.MESH
LOG2E = math.log2(math.e)
VMEM_LIMIT = 60 * 1024 * 1024

TOK = 192
HEAD = 128
MEMBERS = 6
QW = MEMBERS * HEAD
SCORE_SCALE = LOG2E / math.sqrt(HEAD)
BIAS_SCALE = LOG2E / DISTANCE_SCALE

KV_PARTS = 4
KV_ROWS = TOK // KV_PARTS


def flip(value, low, high):
    value = value + low * (1 - 2 * (value % 2))
    return value + high * (3 - 2 * value)


def seq_peer(seq, moves):
    y, x, z = seq // 8, (seq // 2) % 4, seq % 2
    y = flip(y, moves[2], moves[3])
    x = flip(x, moves[0], moves[1])
    z = z + moves[4] * (1 - 2 * z)
    return (y * 4 + x) * 2 + z


def one_move(seq, direction):
    return seq_peer(seq, [1 if d == direction else 0 for d in range(5)])


def kv_mask(part, place, z):
    bits = [(place >> ((d - part) % 4)) & 1 for d in range(4)]
    x = bits[0] ^ (3 * bits[1])
    y = bits[2] ^ (3 * bits[3])
    return (y << 3) | (x << 1) | z


KV_MASKS = np.array(
    [[[kv_mask(q, p, z) for z in range(2)] for q in range(KV_PARTS)] for p in range(16)], np.int32
)


def enter(peers):
    barrier = pltpu.get_barrier_semaphore()
    for peer in peers:
        pl.semaphore_signal(barrier, inc=1, device_id=peer, device_id_type=MESH)
    pl.semaphore_wait(barrier, len(peers))


def send(src, dst, send_sem, recv_sem, peer):
    return pltpu.make_async_remote_copy(
        src_ref=src,
        dst_ref=dst,
        send_sem=send_sem,
        recv_sem=recv_sem,
        device_id=peer,
        device_id_type=MESH,
    )


NT = (((1,), (1,)), ((), ()))
TN = (((0,), (0,)), ((), ()))


def dot_nt(a, b):
    return lax.dot_general(a, b, NT, preferred_element_type=jnp.float32)


def dot_tn(a, b):
    return lax.dot_general(a, b, TN, preferred_element_type=jnp.float32)


def dot_nn(a, b):
    return jnp.dot(a, b, preferred_element_type=jnp.float32)


EDGE = 16
CH = 48


def gelu_value(inputs):
    return (
        0.5 * inputs * (1.0 + jnp.tanh(ROOT_TWO_PI * (inputs + CUBIC * inputs * inputs * inputs)))
    )


def gelu_slope(inputs):
    inner = jnp.tanh(ROOT_TWO_PI * (inputs + CUBIC * inputs * inputs * inputs))
    return 0.5 * (1.0 + inner) + 0.5 * inputs * (1.0 - inner * inner) * ROOT_TWO_PI * (
        1.0 + 3.0 * CUBIC * inputs * inputs
    )


def inverse_rms(values):
    return lax.rsqrt(jnp.mean(values * values, axis=-1, keepdims=True) + EPSILON)


def unpack_bases(words):
    lane = lax.broadcasted_iota(jnp.int32, (TOK, HEAD), 1)
    shift, letter = 2 * ((lane // 4) % 16), lane % 4
    blocks = []
    for j in range(4):
        word = jnp.where(lane < 64, words[:, 2 * j : 2 * j + 1], words[:, 2 * j + 1 : 2 * j + 2])
        field = jnp.bitwise_and(jnp.right_shift(word, shift), 3)
        blocks.append((field == letter).astype(jnp.float32))
    return jnp.concatenate(blocks, axis=1)


def halo(edge_ref, sems, seq):
    after = {"seq": (seq + 1) % 32}
    before = {"seq": (seq + 31) % 32}
    (send_a, recv_a), (send_b, recv_b) = sems
    return [
        send(edge_ref.at[pl.ds(TOK, EDGE)], edge_ref.at[pl.ds(0, EDGE)], send_a, recv_a, after),
        send(
            edge_ref.at[pl.ds(EDGE, EDGE)],
            edge_ref.at[pl.ds(EDGE + TOK, EDGE)],
            send_b,
            recv_b,
            before,
        ),
    ]


def with_edges(edge_ref, seq):
    blank = jnp.zeros((EDGE, QW), jnp.bfloat16)
    head_rows = jnp.where(seq > 0, edge_ref[0:EDGE], blank)
    tail_rows = jnp.where(seq < 31, edge_ref[EDGE + TOK :], blank)
    return jnp.concatenate([head_rows, edge_ref[EDGE : EDGE + TOK], tail_rows], axis=0)


def forward_kernel(
    slope_ref, words_ref, emb_w_ref, cot_ref, qpos_ref, kpos_ref, cw_hbm, qw_hbm, kvw_hbm, ow_hbm,
    att_ref, stat_ref, held_ref, q_ref, back_ref, hidden_ref, embedded_ref, edge_ref,
    normed_t_ref, cot_t_ref,
    cw_ref, qw_ref, kvw_ref, ow_ref, cot_full, kv_ref, normed_ref, acc_ref, top_ref,
    load_sem, send_sem, recv_sem, zsend_sem, zrecv_sem, msend_sem, mrecv_sem,
):
    seq, tp = lax.axis_index("seq"), lax.axis_index("tp")
    loads = []
    for i, (far, near) in enumerate(
        ((ow_hbm, ow_ref), (cw_hbm, cw_ref), (qw_hbm, qw_ref), (kvw_hbm, kvw_ref))
    ):
        loads.append(pltpu.make_async_copy(far, near, load_sem.at[i]))
        loads[i].start()
    peers = [{"seq": one_move(seq, d)} for d in range(5)]
    side = {"tp": 1 - tp}
    enter(peers + [side, {"seq": (seq + 1) % 32}, {"seq": (seq + 31) % 32}])
    mine = pl.ds(pl.multiple_of(tp * QW, HEAD), QW)
    cot_copy = send(cot_ref, cot_full.at[:, mine], msend_sem.at[0], mrecv_sem.at[0], side)
    cot_copy.start()
    patches = unpack_bases(words_ref[...]).astype(jnp.bfloat16)
    embedded = dot_nn(patches, emb_w_ref[...]).astype(jnp.bfloat16)
    embedded_ref[...] = embedded
    embedded_wide = embedded.astype(jnp.float32)
    activated = gelu_value(embedded_wide * inverse_rms(embedded_wide))
    edge_ref[EDGE : EDGE + TOK] = activated.astype(jnp.bfloat16)
    edges = halo(
        edge_ref,
        ((msend_sem.at[1], mrecv_sem.at[1]), (msend_sem.at[2], mrecv_sem.at[2])),
        seq,
    )
    for copy in edges:
        copy.start()
    cot_full[:, mine] = cot_ref[...]
    cot_copy.wait()
    loads[0].wait()
    back_ref[...] = dot_nt(cot_full[...], ow_ref[...]).astype(jnp.bfloat16)
    for copy in edges:
        copy.wait()
    loads[1].wait()
    padded = with_edges(edge_ref, seq)
    hidden = embedded_ref[...].astype(jnp.float32)
    for tap in range(5):
        moved = dot_nn(padded, cw_ref[tap])
        hidden = hidden + moved[EDGE - 2 + tap : EDGE - 2 + tap + TOK]
    hidden_ref[:, mine] = hidden.astype(jnp.bfloat16)
    hidden_copy = send(
        hidden_ref.at[:, mine], hidden_ref.at[:, mine], msend_sem.at[3], mrecv_sem.at[3], side
    )
    hidden_copy.start()
    acc_ref[...] = jnp.zeros_like(acc_ref)
    top_ref[...] = jnp.full_like(top_ref, -1e30)
    hidden_copy.wait()
    loads[2].wait()
    loads[3].wait()
    hidden_wide = hidden_ref[...].astype(jnp.float32)
    normed_ref[...] = (hidden_wide * inverse_rms(hidden_wide)).astype(jnp.bfloat16)
    kv_ref[...] = dot_nn(normed_ref[...], kvw_ref[...]).astype(jnp.bfloat16)
    zcopies = []
    for part in range(KV_PARTS):
        rows = pl.ds(part * KV_ROWS, KV_ROWS)
        copy = send(
            kv_ref.at[rows],
            held_ref.at[0, part, pl.ds(KV_ROWS, KV_ROWS)],
            zsend_sem.at[part],
            zrecv_sem.at[part],
            peers[4],
        )
        copy.start()
        zcopies.append(copy)
    for part in range(KV_PARTS):
        held_ref[0, part, 0:KV_ROWS] = kv_ref[part * KV_ROWS : (part + 1) * KV_ROWS]
    q_ref[...] = dot_nn(normed_ref[...], qw_ref[...]).astype(jnp.bfloat16)
    qpos = qpos_ref[...]

    def absorb(pair, kpos):
        keys = pair[:, :HEAD]
        values = jnp.concatenate([pair[:, HEAD:], jnp.ones_like(keys)], axis=1)
        distance = jnp.abs(qpos - kpos)
        for head in range(MEMBERS):
            scores = dot_nt(q_ref[:, head * HEAD : (head + 1) * HEAD], keys) * SCORE_SCALE
            scores = scores - distance * (slope_ref[head] * BIAS_SCALE)
            old = top_ref[head]
            new = jnp.maximum(old, jnp.max(scores, axis=1, keepdims=True))
            fading = jnp.exp2(old - new)
            weights = jnp.exp2(scores - new[:, :1]).astype(jnp.bfloat16)
            acc_ref[head] = acc_ref[head] * jnp.concatenate([fading, fading], axis=1) + dot_nn(
                weights, values
            )
            top_ref[head] = new

    def places(first, count):
        pair = held_ref[pl.ds(first, count)].reshape(count * 2 * TOK, 2 * HEAD)
        if count == 1:
            kpos = kpos_ref[first]
        else:
            kpos = jnp.concatenate([kpos_ref[first + i] for i in range(count)], axis=1)
        absorb(pair, kpos)

    def start_stage(k):
        copies = []
        for part in range(KV_PARTS):
            copy = send(
                held_ref.at[pl.ds(0, 2**k), part],
                held_ref.at[pl.ds(2**k, 2**k), part],
                send_sem.at[k, part],
                recv_sem.at[k, part],
                peers[(part + k) % 4],
            )
            copy.start()
            copies.append(copy)
        return copies

    def turned(ref, target, first, count):
        columns = slice(first * 2 * CH * 4, (first + count) * 2 * CH * 4)
        block = ref[:, columns].astype(jnp.float32).T.astype(jnp.bfloat16)
        target[8 * first : 8 * (first + count)] = block.reshape(8 * count, CH, TOK)

    for copy in zcopies:
        copy.wait()
    stage = start_stage(0)
    places(0, 1)
    for copy in stage:
        copy.wait()
    stage = start_stage(1)
    places(1, 1)
    turned(normed_ref, normed_t_ref, 0, 1)
    for copy in stage:
        copy.wait()
    stage = start_stage(2)
    places(2, 2)
    turned(normed_ref, normed_t_ref, 1, 2)
    for copy in stage:
        copy.wait()
    stage = start_stage(3)

    def two_places(first):
        def step(i, carry):
            places(first + 2 * i, 2)
            return carry

        return step

    lax.fori_loop(0, 2, two_places(4), 0)
    turned(normed_ref, normed_t_ref, 3, 1)
    turned(cot_full, cot_t_ref, 0, 4)
    for copy in stage:
        copy.wait()
    lax.fori_loop(0, 4, two_places(8), 0)
    lane = lax.broadcasted_iota(jnp.int32, (TOK, HEAD), 1)
    stats = jnp.zeros((TOK, HEAD), jnp.float32)
    for head in range(MEMBERS):
        totals = acc_ref[head, :, HEAD:]
        mixed = (acc_ref[head, :, :HEAD] / totals).astype(jnp.bfloat16)
        att_ref[:, head * HEAD : (head + 1) * HEAD] = mixed
        back = back_ref[:, head * HEAD : (head + 1) * HEAD].astype(jnp.float32)
        delta = jnp.sum(back * mixed.astype(jnp.float32), axis=1, keepdims=True)
        stats = jnp.where(lane == head, top_ref[head] + jnp.log2(totals), stats)
        stats = jnp.where(lane == 8 + head, delta, stats)
    stat_ref[...] = stats


def forward_attention(*operands):
    vmem = pl.BlockSpec(memory_space=pltpu.VMEM)
    f32, bf16 = jnp.float32, jnp.bfloat16
    return pl.pallas_call(
        forward_kernel,
        out_shape=(
            jax.ShapeDtypeStruct((TOK, QW), bf16),
            jax.ShapeDtypeStruct((TOK, HEAD), f32),
            jax.ShapeDtypeStruct((16, KV_PARTS, 2 * KV_ROWS, 2 * HEAD), bf16),
            jax.ShapeDtypeStruct((TOK, QW), bf16),
            jax.ShapeDtypeStruct((TOK, QW), bf16),
            jax.ShapeDtypeStruct((TOK, 2 * QW), bf16),
            jax.ShapeDtypeStruct((TOK, QW), bf16),
            jax.ShapeDtypeStruct((TOK + 2 * EDGE, QW), bf16),
            jax.ShapeDtypeStruct((32, CH, TOK), bf16),
            jax.ShapeDtypeStruct((32, CH, TOK), bf16),
        ),
        in_specs=[pl.BlockSpec(memory_space=pltpu.SMEM)]
        + [vmem] * 5
        + [pl.BlockSpec(memory_space=pl.ANY)] * 4,
        out_specs=(vmem,) * 10,
        scratch_shapes=[
            pltpu.VMEM((5, QW, QW), bf16),
            pltpu.VMEM((2 * QW, QW), bf16),
            pltpu.VMEM((2 * QW, 2 * HEAD), bf16),
            pltpu.VMEM((QW, 2 * QW), bf16),
            pltpu.VMEM((TOK, 2 * QW), bf16),
            pltpu.VMEM((TOK, 2 * HEAD), bf16),
            pltpu.VMEM((TOK, 2 * QW), bf16),
            pltpu.VMEM((MEMBERS, TOK, 2 * HEAD), f32),
            pltpu.VMEM((MEMBERS, TOK, HEAD), f32),
            pltpu.SemaphoreType.DMA((4,)),
            pltpu.SemaphoreType.DMA((4, KV_PARTS)),
            pltpu.SemaphoreType.DMA((4, KV_PARTS)),
            pltpu.SemaphoreType.DMA((KV_PARTS,)),
            pltpu.SemaphoreType.DMA((KV_PARTS,)),
            pltpu.SemaphoreType.DMA((4,)),
            pltpu.SemaphoreType.DMA((4,)),
        ],
        compiler_params=pltpu.CompilerParams(
            collective_id=0, has_side_effects=True, vmem_limit_bytes=VMEM_LIMIT
        ),
    )(*operands)


def backward_kernel(
    kbase_ref, q_ref, back_ref, held_ref, qpos_ref, slope_ref, lse_ref, delta_ref,
    dq_ref, dkv_ref,
    qs_ref, bs_ref, dq_acc, part_ref, land3, land2, land1, land0, landz,
    send_sem, recv_sem, zsend_sem, zrecv_sem,
):
    seq = lax.axis_index("seq")
    peers = [{"seq": one_move(seq, d)} for d in range(5)]
    enter(peers)
    lands = [land0, land1, land2, land3]
    for head in range(MEMBERS):
        rows = slice(head * TOK, (head + 1) * TOK)
        qs_ref[rows] = q_ref[:, head * HEAD : (head + 1) * HEAD]
        bs_ref[rows] = back_ref[:, head * HEAD : (head + 1) * HEAD]
    dq_acc[...] = jnp.zeros_like(dq_acc)
    qpos = qpos_ref[...]
    row = lax.broadcasted_iota(jnp.int32, (KV_ROWS, 1), 0).astype(jnp.float32)

    def one_place(place, carry):
        pair = held_ref[place].reshape(2 * TOK, 2 * HEAD)
        keys, values = pair[:, :HEAD], pair[:, HEAD:]
        kpos = jnp.concatenate([row + kbase_ref[place, g] for g in range(8)], axis=0)
        distance = jnp.abs(qpos - kpos)
        key_grad = jnp.zeros((2 * TOK, HEAD), jnp.float32)
        value_grad = jnp.zeros((2 * TOK, HEAD), jnp.float32)
        for duo in range(MEMBERS // 2):
            rows = slice(duo * 2 * TOK, (duo + 1) * 2 * TOK)
            qd, bd = qs_ref[rows], bs_ref[rows]
            scores = dot_nt(keys, qd) * SCORE_SCALE - distance * slope_ref[duo]
            probs = jnp.exp2(scores - lse_ref[duo])
            back_probs = dot_nt(values, bd)
            grad_scores = (probs * (back_probs - delta_ref[duo])).astype(jnp.bfloat16)
            value_grad = value_grad + dot_nn(probs.astype(jnp.bfloat16), bd)
            key_grad = key_grad + dot_nn(grad_scores, qd)
            dq_acc[rows] += dot_tn(grad_scores, keys)
        both = jnp.concatenate([key_grad * (1.0 / math.sqrt(HEAD)), value_grad], axis=1)
        part_ref[place] = both.astype(jnp.bfloat16).reshape(KV_PARTS, 2 * KV_ROWS, 2 * HEAD)
        return carry

    def start_stage(k):
        copies = []
        for part in range(KV_PARTS):
            copy = send(
                part_ref.at[pl.ds(2**k, 2**k), part],
                lands[k].at[pl.ds(0, 2**k), part],
                send_sem.at[k, part],
                recv_sem.at[k, part],
                peers[(part + k) % 4],
            )
            copy.start()
            copies.append(copy)
        return copies

    def take_in(low, high, copies, stage):
        for copy in copies:
            copy.wait()

        def add(p, carry):
            total = part_ref[p].astype(jnp.float32)
            for k in range(stage, 4):
                total = total + lands[k][p].astype(jnp.float32)
            part_ref[p] = total.astype(jnp.bfloat16)
            return carry

        lax.fori_loop(low, high, add, 0)

    lax.fori_loop(8, 16, one_place, 0)
    copies = start_stage(3)
    for k in (2, 1, 0):
        lax.fori_loop(2**k, 2 ** (k + 1), one_place, 0)
        take_in(2**k, 2 ** (k + 1), copies, k + 1)
        copies = start_stage(k)
    lax.fori_loop(0, 1, one_place, 0)
    take_in(0, 1, copies, 0)
    zcopies = []
    for part in range(KV_PARTS):
        copy = send(
            part_ref.at[0, part, pl.ds(KV_ROWS, KV_ROWS)],
            landz.at[part],
            zsend_sem.at[part],
            zrecv_sem.at[part],
            peers[4],
        )
        copy.start()
        zcopies.append(copy)
    for head in range(MEMBERS):
        grad = dq_acc[head * TOK : (head + 1) * TOK] * (1.0 / math.sqrt(HEAD))
        dq_ref[:, head * HEAD : (head + 1) * HEAD] = grad.astype(jnp.bfloat16)
    for part in range(KV_PARTS):
        zcopies[part].wait()
        dkv_ref[part * KV_ROWS : (part + 1) * KV_ROWS] = part_ref[0, part, 0:KV_ROWS] + landz[part]


def backward_attention(kbase, queries, back_attended, held, qpos, slopes, lse, delta):
    vmem = pl.BlockSpec(memory_space=pltpu.VMEM)
    block = (KV_PARTS, 2 * KV_ROWS, 2 * HEAD)
    return pl.pallas_call(
        backward_kernel,
        out_shape=(
            jax.ShapeDtypeStruct((TOK, QW), jnp.bfloat16),
            jax.ShapeDtypeStruct((TOK, 2 * HEAD), jnp.bfloat16),
        ),
        in_specs=[pl.BlockSpec(memory_space=pltpu.SMEM)] + [vmem] * 7,
        out_specs=(vmem, vmem),
        scratch_shapes=[
            pltpu.VMEM((MEMBERS * TOK, HEAD), jnp.bfloat16),
            pltpu.VMEM((MEMBERS * TOK, HEAD), jnp.bfloat16),
            pltpu.VMEM((MEMBERS * TOK, HEAD), jnp.float32),
            pltpu.VMEM((16,) + block, jnp.bfloat16),
            pltpu.VMEM((8,) + block, jnp.bfloat16),
            pltpu.VMEM((4,) + block, jnp.bfloat16),
            pltpu.VMEM((2,) + block, jnp.bfloat16),
            pltpu.VMEM((1,) + block, jnp.bfloat16),
            pltpu.VMEM((KV_PARTS, KV_ROWS, 2 * HEAD), jnp.bfloat16),
            pltpu.SemaphoreType.DMA((4, KV_PARTS)),
            pltpu.SemaphoreType.DMA((4, KV_PARTS)),
            pltpu.SemaphoreType.DMA((KV_PARTS,)),
            pltpu.SemaphoreType.DMA((KV_PARTS,)),
        ],
        compiler_params=pltpu.CompilerParams(
            collective_id=1, has_side_effects=True, vmem_limit_bytes=VMEM_LIMIT
        ),
    )(kbase, queries, back_attended, held, qpos, slopes, lse, delta)


HALF = QW // 2
WIDTHS = (HALF, HALF, HALF, HALF, 2 * HEAD, HALF, HALF, HALF, HALF, HALF, HEAD)
TURNS = (2, 3, 0, 1, 4, 0, 1, 2, 3, 4, 4)
EARLY = (2, 3, 0, 1, 4)
LATE = (5, 6, 7, 8, 9)
EMBED = 10

def weights_kernel(
    normed_ref, cot_ref, act_ref, words_ref,
    dq_ref, att_ref, pair_ref, hidden_ref, embedded_ref, cotangent_ref,
    cw_hbm, qw_hbm, kvw_hbm, ow_hbm,
    result_out, query_out, output_out, pair_out, conv_out, embed_out,
    *scratch, factor,
):
    sums, lands, dp_lands = scratch[:11], scratch[11:22], scratch[22:33]
    (
        cw_ref, qw_ref, kvw_ref, ow_ref, win_ref, patch_ref, out_own, out_side,
        wide_own, wide_side, edge_ref, conv_side, active_own, active_side, emb_ref,
        land_tp, land_diag, load_sem, send_sem, recv_sem, fsend_sem, frecv_sem,
    ) = scratch[33:]
    seq, dp, tp = lax.axis_index("seq"), lax.axis_index("dp"), lax.axis_index("tp")
    loads = []
    for i, (far, near) in enumerate(
        ((qw_hbm, qw_ref), (kvw_hbm, kvw_ref), (ow_hbm, ow_ref), (cw_hbm, cw_ref))
    ):
        loads.append(pltpu.make_async_copy(far, near, load_sem.at[i]))
        loads[i].start()
    peers = [{"seq": one_move(seq, d)} for d in range(5)]
    over = {"dp": 1 - dp}
    side = {"tp": 1 - tp}
    diagonal = {"dp": 1 - dp, "tp": 1 - tp}
    around = [{"seq": (seq + 1) % 32}, {"seq": (seq + 31) % 32}]
    enter(peers + [over, side, diagonal] + around)
    upper = lax.broadcasted_iota(jnp.int32, (16 * CH, HALF), 0) % CH < CH // 2

    def fill(part, half):
        turn = TURNS[part]
        where = []
        for place in range(16 * half, 16 * half + 16):
            bits = [(place >> ((d - turn) % 5)) & 1 for d in range(5)]
            where.append(seq_peer(seq, bits))

        def rows(ref, start, count):
            return jnp.concatenate([ref[w, start : start + count] for w in where], axis=0)

        conv = slice(EDGE, EDGE + TOK)
        if part < 2:
            grads = dot_nn(rows(normed_ref, 0, CH), dq_ref[:, part * HALF : (part + 1) * HALF])
        elif part < 4:
            columns = slice((part - 2) * HALF, (part - 1) * HALF)
            grads = dot_nn(rows(cot_ref, 0, CH), att_ref[:, columns])
        elif part == 4:
            grads = dot_nn(rows(normed_ref, 0, CH), pair_ref[...])
        elif part < 9:
            column = (part - 5) % 2 * HALF
            chosen = rows(win_ref.at[(part - 5) // 2], 0, CH)
            grads = dot_nn(chosen, edge_ref[conv, column : column + HALF])
        elif part == 9:
            chosen = rows(win_ref.at[2], 0, CH)
            left = dot_nn(chosen, edge_ref[conv, :HALF])
            grads = jnp.where(upper, left, dot_nn(chosen, edge_ref[conv, HALF:]))
        else:
            columns = pl.ds(pl.multiple_of(tp * HALF, HEAD), HALF)
            emb = dot_nn(rows(patch_ref, 0, 16), emb_ref[:, columns])
            grads = jnp.concatenate(
                [
                    emb[16 * j : 16 * j + 16, HEAD * c : HEAD * c + HEAD]
                    for j in range(16)
                    for c in range(3)
                ],
                axis=0,
            )
        sums[part][16 * half : 16 * half + 16] = grads.astype(jnp.bfloat16).reshape(
            16, CH, WIDTHS[part]
        )

    def start(part, k):
        copies = []
        if k > 0:
            spans = ((2 ** (k - 1), 2 ** (k - 1)), (0, 2 ** (k - 1)))
        else:
            spans = ((0, 1),)
        for piece, (low, count) in enumerate(spans):
            copy = send(
                sums[part].at[pl.ds(2**k + low, count)],
                lands[part].at[pl.ds(2**k + low, count)],
                send_sem.at[part, k, piece],
                recv_sem.at[part, k, piece],
                peers[(TURNS[part] + k) % 5],
            )
            copy.start()
            copies.append((copy, low, count))
        return copies

    def settle(part, k, item):
        copy, low, count = item
        copy.wait()
        bunch = min(count, 4)

        def add(i, carry):
            at = pl.ds(low + i * bunch, bunch)
            sums[part][at] = sums[part][at] + lands[part][pl.ds(2**k + low + i * bunch, bunch)]
            return carry

        lax.fori_loop(0, count // bunch, add, 0)

    flights = {}

    def launch(parts):
        for part in parts:
            flights[part] = start(part, 4)

    def advance(parts, k):
        following = {}
        for part in parts:
            settle(part, k, flights[part][0])
            following[part] = start(part, k - 1)
        for part in parts:
            settle(part, k, flights[part][1])
        flights.update(following)

    finals = {}

    def finish(parts):
        for part in parts:
            settle(part, 0, flights[part][0])
            copy = send(
                sums[part].at[0], dp_lands[part], fsend_sem.at[part], frecv_sem.at[part], over
            )
            copy.start()
            finals[part] = copy

    def total(part):
        finals[part].wait()
        return (sums[part][0].astype(jnp.float32) + dp_lands[part][...].astype(jnp.float32)) * factor

    for part in EARLY:
        fill(part, 1)
        launch([part])
    loads[0].wait()
    loads[1].wait()
    partial = dot_nt(dq_ref[...], qw_ref[...]) + dot_nt(pair_ref[...], kvw_ref[...])
    wide_own[...] = partial.astype(jnp.bfloat16)
    wide_copy = send(wide_own, wide_side, fsend_sem.at[11], frecv_sem.at[11], side)
    wide_copy.start()
    padded = with_edges(act_ref, seq).astype(jnp.float32)
    turned = []
    for tap in range(5):
        window = padded[EDGE - 2 + tap : EDGE - 2 + tap + TOK].T
        turned.append(window.reshape(32, CH // 2, TOK))
    for i, pair in enumerate(((0, 1), (2, 3), (4, 4))):
        both = jnp.concatenate([turned[tap] for tap in pair], axis=1)
        win_ref[i] = both.astype(jnp.bfloat16)
    hidden = hidden_ref[...].astype(jnp.float32)
    scale = inverse_rms(hidden)
    wide_copy.wait()
    back_normed = wide_own[...].astype(jnp.float32) + wide_side[...].astype(jnp.float32)
    mean = jnp.mean(back_normed * (hidden * scale), axis=-1, keepdims=True)
    mine = pl.ds(pl.multiple_of(tp * QW, HEAD), QW)
    own = wide_own[:, mine].astype(jnp.float32) + wide_side[:, mine].astype(jnp.float32)
    normed = hidden_ref[:, mine].astype(jnp.float32) * scale
    back_hidden = cotangent_ref[...].astype(jnp.float32) + scale * (own - normed * mean)
    edge_ref[EDGE : EDGE + TOK] = back_hidden.astype(jnp.bfloat16)
    edge_copies = halo(
        edge_ref,
        ((fsend_sem.at[12], frecv_sem.at[12]), (fsend_sem.at[13], frecv_sem.at[13])),
        seq,
    )
    for copy in edge_copies:
        copy.start()
    conv_copy = send(
        edge_ref.at[pl.ds(EDGE, TOK)], conv_side, fsend_sem.at[14], frecv_sem.at[14], side
    )
    conv_copy.start()
    for part in LATE:
        fill(part, 1)
        launch([part])
    loads[3].wait()
    for copy in edge_copies:
        copy.wait()
    padded = with_edges(edge_ref, seq)
    active = jnp.zeros((TOK, QW), jnp.float32)
    for tap in range(5):
        moved = dot_nt(padded, cw_ref[tap])
        active = active + moved[EDGE + 2 - tap : EDGE + 2 - tap + TOK]
    active_own[...] = active.astype(jnp.bfloat16)
    active_copy = send(active_own, active_side, fsend_sem.at[15], frecv_sem.at[15], side)
    active_copy.start()
    loads[2].wait()
    out_own[...] = dot_nn(att_ref[...], ow_ref[...]).astype(jnp.bfloat16)
    theirs = pl.ds(pl.multiple_of((1 - tp) * QW, HEAD), QW)
    out_copy = send(out_own.at[:, theirs], out_side, fsend_sem.at[18], frecv_sem.at[18], side)
    out_copy.start()
    patches = unpack_bases(words_ref[...]).T
    patch_ref[...] = patches.reshape(32, 16, TOK).astype(jnp.bfloat16)
    embedded = embedded_ref[...].astype(jnp.float32)
    scale_in = inverse_rms(embedded)
    normed_in = embedded * scale_in
    slope = gelu_slope(normed_in)
    conv_copy.wait()
    residual = edge_ref[EDGE : EDGE + TOK].astype(jnp.float32) + conv_side[...].astype(jnp.float32)
    active_copy.wait()
    back_in = (active_own[...].astype(jnp.float32) + active_side[...].astype(jnp.float32)) * slope
    mean_in = jnp.mean(back_in * normed_in, axis=-1, keepdims=True)
    emb_ref[...] = (residual + scale_in * (back_in - normed_in * mean_in)).astype(jnp.bfloat16)
    fill(EMBED, 1)
    launch([EMBED])
    for part in EARLY + LATE + (EMBED,):
        fill(part, 0)
    out_copy.wait()
    projected = out_own[:, mine].astype(jnp.float32) + out_side[...].astype(jnp.float32)
    result_out[...] = (hidden_ref[:, mine].astype(jnp.float32) + projected).astype(jnp.bfloat16)
    late = LATE + (EMBED,)
    for k in (4, 3, 2, 1):
        advance(EARLY, k)
        advance(late, k)
    finish(EARLY)
    finish(late)
    sidecopy = send(sums[EMBED].at[0], land_tp, fsend_sem.at[16], frecv_sem.at[16], side)
    sidecopy.start()
    diagcopy = send(sums[EMBED].at[0], land_diag, fsend_sem.at[17], frecv_sem.at[17], diagonal)
    diagcopy.start()
    for half in range(2):
        query_out[:, half * HALF : (half + 1) * HALF] = total(half)
    for half in range(2):
        output_out[half * HALF : (half + 1) * HALF, :] = total(2 + half).T
    pair_out[...] = total(4)
    rows = CH // 2
    for part in range(4):
        tap, columns = part // 2 * 2, slice(part % 2 * HALF, (part % 2 + 1) * HALF)
        block = total(5 + part)
        conv_out[tap, :, columns] = block[:rows]
        conv_out[tap + 1, :, columns] = block[rows:]
    block = total(9)
    conv_out[4, :, :HALF] = block[:rows]
    conv_out[4, :, HALF:] = block[rows:]

    def embed_store(block, core):
        wide = jnp.concatenate([block[:16], block[16:32], block[32:]], axis=1)
        embed_out[:, pl.ds(pl.multiple_of(core * HALF, HEAD), HALF)] = wide

    embed_store(total(EMBED), tp)
    sidecopy.wait()
    diagcopy.wait()
    other = land_tp[...].astype(jnp.float32) + land_diag[...].astype(jnp.float32)
    embed_store(other * factor, 1 - tp)


def weight_gradients(factor, *operands):
    vmem = pl.BlockSpec(memory_space=pltpu.VMEM)
    f32, bf16 = jnp.float32, jnp.bfloat16
    return pl.pallas_call(
        functools.partial(weights_kernel, factor=factor),
        out_shape=(
            jax.ShapeDtypeStruct((TOK, QW), bf16),
            jax.ShapeDtypeStruct((CH, QW), f32),
            jax.ShapeDtypeStruct((QW, CH), f32),
            jax.ShapeDtypeStruct((CH, 2 * HEAD), f32),
            jax.ShapeDtypeStruct((5, CH // 2, QW), f32),
            jax.ShapeDtypeStruct((16, QW), f32),
        ),
        in_specs=[vmem] * 10 + [pl.BlockSpec(memory_space=pl.ANY)] * 4,
        out_specs=(vmem,) * 6,
        scratch_shapes=[pltpu.VMEM((32, CH, w), bf16) for w in WIDTHS]
        + [pltpu.VMEM((32, CH, w), bf16) for w in WIDTHS]
        + [pltpu.VMEM((CH, w), bf16) for w in WIDTHS]
        + [
            pltpu.VMEM((5, QW, QW), bf16),
            pltpu.VMEM((2 * QW, QW), bf16),
            pltpu.VMEM((2 * QW, 2 * HEAD), bf16),
            pltpu.VMEM((QW, 2 * QW), bf16),
            pltpu.VMEM((3, 32, CH, TOK), bf16),
            pltpu.VMEM((32, 16, TOK), bf16),
            pltpu.VMEM((TOK, 2 * QW), bf16),
            pltpu.VMEM((TOK, QW), bf16),
            pltpu.VMEM((TOK, 2 * QW), bf16),
            pltpu.VMEM((TOK, 2 * QW), bf16),
            pltpu.VMEM((TOK + 2 * EDGE, QW), bf16),
            pltpu.VMEM((TOK, QW), bf16),
            pltpu.VMEM((TOK, QW), bf16),
            pltpu.VMEM((TOK, QW), bf16),
            pltpu.VMEM((TOK, QW), bf16),
            pltpu.VMEM((CH, HEAD), bf16),
            pltpu.VMEM((CH, HEAD), bf16),
            pltpu.SemaphoreType.DMA((4,)),
            pltpu.SemaphoreType.DMA((11, 5, 2)),
            pltpu.SemaphoreType.DMA((11, 5, 2)),
            pltpu.SemaphoreType.DMA((19,)),
            pltpu.SemaphoreType.DMA((19,)),
        ],
        compiler_params=pltpu.CompilerParams(
            collective_id=2, has_side_effects=True, vmem_limit_bytes=VMEM_LIMIT
        ),
    )(*operands)


def per_device(
    bases,
    shifts,
    embed_weight,
    conv_weight,
    query_weight,
    keyvalue_weight,
    output_weight,
    slopes,
    cotangent,
):
    tokens = cotangent.shape[1]
    seq = lax.axis_index("seq")
    seq_count = lax.axis_size("seq")
    words = bases.reshape(tokens, -1)
    pair_weight = keyvalue_weight.reshape(2 * QW, 2 * HEAD)
    cotangent_local = cotangent[0]
    token = jnp.arange(tokens, dtype=jnp.int32)
    qpos = (seq * tokens + token + shifts[0]).astype(jnp.float32)
    sources = jnp.bitwise_xor(seq, KV_MASKS) * tokens
    kbase = sources + (KV_ROWS * np.arange(KV_PARTS, dtype=np.int32))[None, :, None]
    kbase = kbase.reshape(16, 2 * KV_PARTS)
    kpos = kbase[:, :, None] + jnp.arange(KV_ROWS, dtype=jnp.int32)
    kpos = kpos.reshape(16, 1, 2 * tokens).astype(jnp.float32)
    (
        attended, stats, held, queries, back_attended, hidden, embedded, edges, normed_t, cot_t
    ) = forward_attention(
        slopes,
        words,
        embed_weight,
        cotangent_local,
        qpos.reshape(tokens, 1),
        kpos,
        conv_weight,
        query_weight,
        pair_weight,
        output_weight,
    )
    lse = stats[:, :MEMBERS].T.reshape(MEMBERS // 2, 1, 2 * tokens)
    delta = stats[:, 8 : 8 + MEMBERS].T.reshape(MEMBERS // 2, 1, 2 * tokens)
    slope_rows = jnp.repeat(slopes * BIAS_SCALE, tokens).reshape(MEMBERS // 2, 1, 2 * tokens)
    back_query, back_pair = backward_attention(
        kbase.astype(jnp.float32),
        queries,
        back_attended,
        held,
        jnp.tile(qpos, 2).reshape(1, 2 * tokens),
        slope_rows,
        lse,
        delta,
    )
    factor = (lax.axis_size("dp") * seq_count * tokens) ** (-0.5)
    result, grad_query, grad_output, grad_pair, grad_conv, grad_embed = weight_gradients(
        factor,
        normed_t,
        cot_t,
        edges,
        words,
        back_query,
        attended,
        back_pair,
        hidden,
        embedded,
        cotangent_local,
        conv_weight,
        query_weight,
        pair_weight,
        output_weight,
    )
    grad_pair = grad_pair.reshape(CH, 1, 2 * HEAD)
    return (result[None], grad_embed, grad_conv, grad_query, grad_pair, grad_output)


def solution(mesh):
    placed = (
        P("dp", "seq"),
        P("dp"),
        P(),
        P(None, None, "tp"),
        P(None, "tp"),
        P(None, "tp", None),
        P("tp", None),
        P("tp"),
        P("dp", "seq", "tp"),
    )
    return jax.shard_map(
        per_device,
        mesh=mesh,
        in_specs=placed,
        out_specs=(
            P("dp", "seq", "tp"),
            P("seq", None),
            P(None, "seq", "tp"),
            P("seq", "tp"),
            P("seq", "tp", None),
            P("tp", "seq"),
        ),
        check_vma=False,
    )
```

time: 271 us -> 193 us (0.71)
  matrix products: 23.6 us -> 0 us
  starting transfers between devices: 20.5 us -> 0 us
  other arithmetic: 23.4 us -> 3.43 us
  local copies, waits for them, and re-layouts: 32.6 us -> 15.5 us
  Pallas kernels: 162 us -> 173 us
  blocking collectives: 5.17 us -> 0 us
    dot_general x9 -> x0, matrix products: 23.6 us -> none  [the longest x1 5.31 us: per_device(): jnp.einsum('tko,kco->tc', back_windows.reshape(tokens, taps_count, local_...]
    ppermute x7 -> x0, starting transfers between devices: 20.5 us -> none  [the longest x2 9.2 us: sequence_rims(): before = lax.ppermute(shard[length - width:], 'seq', up)]
    pallas_call x1, Pallas kernels: 41 us -> 51 us  [forward_attention(): pl.pallas_call(forward_kernel, out_shape=(jax.ShapeDtypeStruct((TOK, QW),...]
    unnamed x42 -> x6, local copies, waits for them, and re-layouts: 1.72 us -> 9.71 us
    concatenate x2 -> x0, local copies, waits for them, and re-layouts: 7.46 us -> none  [the longest x1 3.74 us: per_device(): jnp.concatenate([padded[tap_index:tap_index + tokens] for tap_index in ra...]
    slice x9 -> x0, local copies, waits for them, and re-layouts: 6.82 us -> none  [the longest x2 2.88 us: per_device(): early = by_chunk[:, :4].reshape(seq_count, 4 * rows, tokens)]
    all_gather x2 -> x0, blocking collectives: 5.17 us -> none  [feature_halves(): return lax.all_gather(values, 'tp', axis=1, tiled=True)]
    transpose x3 -> x0, local copies, waits for them, and re-layouts: 5.1 us -> none  [the longest x1 2.22 us: per_device(): normed.T.reshape(seq_count, CH, tokens)]
  transfers between devices with their start and end apart: 7 -> 0, of which waited for: 0 -> 0; matrix products, arithmetic and copies ran while one was open for 17% -> 0% of each run, Pallas kernels for 0% -> 0%
where the time goes in v2:
time: 193 us
  Pallas kernels  173 us (90%)
  local copies, waits for them, and re-layouts  15.5 us (8%)
  other arithmetic  3.43 us (2%)
    pallas_call x1, Pallas kernels, weight_gradients(): pl.pallas_call(functools.partial(weights_kernel, factor=factor), out_shap...  79.3 us
    pallas_call x1, Pallas kernels, forward_attention(): pl.pallas_call(forward_kernel, out_shape=(jax.ShapeDtypeStruct((TOK, QW),...  51 us
    pallas_call x1, Pallas kernels, backward_attention(): pl.pallas_call(backward_kernel, out_shape=(jax.ShapeDtypeStruct((TOK, QW)...  42.2 us
    unnamed x6, local copies, waits for them, and re-layouts  9.71 us

profile of v2, /device:TPU:1, one launch (start us, length us, event | category | flops | bytes accessed | tf_op | source)
XLA Modules:
  0.0 192.9 jit_solution(5558924137808100704)
XLA Ops:
  1.3 0.7 broadcast_multiply_fusion
  2.0 0.6 reshape_tile.3.qpos_ref
  2.6 0.1 broadcast_in_dim.11
  2.7 0.8 multiply_add_fusion
  3.5 0.1 copy.30
  3.5 0.7 copy.33.kbase_ref
  4.2 0.1 broadcast_in_dim.12
  4.3 0.7 broadcast_in_dim.13.slope_ref
  5.0 0.1 add.92
  5.0 0.7 reduce
  5.8 0.1 add.89
  5.8 0.1 add.90
  6.0 0.6 add_convert_fusion.1.kpos_ref
  6.6 0.7 reshape.102.words_ref
  7.3 0.7 add_convert_fusion.qpos_ref
  8.0 51.0 %shard_map.154 = (bf16[192,768]{1,0:T(8,128)(2,1)}, f32[192,128]{1,0:T(8,128)}, bf16[16,4,96,256]{3,2,1,0:T(8,128)(2,1)}, bf16[192,768]{1,0:T(8,128)(2,1)}, bf16...) custom-call(f32[6]{0:T(128)} %slope_ref.1, ...), custom_call_target="tpu_custom_call" | custom-call | tf_op jit(solution)/shard_map/pallas_call | solution.py:314
  59.0 1.1 slice_bitcast_fusion
  60.1 0.1 copy.32
  60.1 0.7 reshape.105.delta_ref
  60.8 0.1 copy.31
  60.9 0.7 reshape.104.lse_ref
  61.6 42.2 %shard_map.155 = (bf16[192,768]{1,0:T(8,128)(2,1)}, bf16[192,256]{1,0:T(8,128)(2,1)}) custom-call(f32[16,8]{1,0:T(8,128)} %copy.33.kbase_ref, bf16[192,768]{1,0:T(8,128)(2,1)} %get-tuple-element.27.q_ref, bf16[192,768]{1,0:T(8,128)(2,1)} %get-tuple-element.28.back_ref, bf16[16,4,96,256]{3,2,1,0:T(8,128)(2,1)} %get-tuple-element.29.held_ref, ...), custom_call_target="tpu_custom_call" | custom-call | tf_op jit(solution)/shard_map/pallas_call | solution.py:452
  103.8 79.3 %shard_map.156 = (bf16[192,768]{1,0:T(8,128)(2,1)}, f32[48,768]{1,0:T(8,128)}, f32[768,48]{1,0:T(8,128)}, f32[48,256]{1,0:T(8,128)}, f32[5,24,768]{2,1,0:T(8,128)}, /*index=5*/f32[16,768]{1,0:T(8,128)}) custom-call(bf16[32,48,192]{2,1,0:T(8,128)(2,1)} %get-tuple-element.24.normed_ref, bf16[32,48,192]{2,1,0:T(8,128)(2,1)} %get-tuple-element.25.cot_ref, ...), custom_call_target="tpu_custom_call" | custom-call | tf_op jit(solution)/shard_map/pallas_call | solution.py:732
  183.1 1.5 copy.34
  184.6 1.8 copy.35
  186.4 1.7 copy.41
  188.1 1.4 copy.42
  189.5 1.7 copy.43
  191.3 1.6 copy.44
  (5 shorter events, 0.0 us)
